TPU v7x, 32 devices: a whole 2x2x4 slice. The times are simulated.
32 devices in a mesh: gx: 4 (over y, x), gy: 8 (over z, core).
Axes of the slice: x: 2, y: 2, z: 4, core: 2. Of those that a mesh axis runs over, the one named last changes fastest.
Arguments:
- white_noise: float32 [4, 4096, 4096], P('gx', 'gy'), may hold values from -6 to 6
- amplitude: float32 [4096, 4096], P(None, 'gy'), may hold values from 0.24 to 1.26, as said below
- offsets: int32 [2], replicated, may hold values from 0 to 7
Outputs:
- trans_x: float32 [4, 4096, 4096], P('gx', 'gy')
- trans_y: float32 [4, 4096, 4096], P('gx', 'gy')
- upscaled: float32 [512, 512], P('gy', 'gx')
Inputs may be any that keep to these rules, and one draw needn't show every extreme that they name: amplitude[ky, kx] equals amplitude[(4096 - ky) mod 4096, kx] and amplitude[ky, (4096 - kx) mod 4096]. offsets[0] shifts the coarse blocks along y, offsets[1] along x.
All inputs are finite; a program needn't handle non-finite values.
Results may differ from a plain program's by a relative error of at most 0.000096.
Values sent between devices are 32-bit elements; how exact they have to be, the bound alone decides.
No kernel may reach another device: no remote copies, remote signals or barrier semaphores. Data moves between devices by JAX's collectives and lax.ppermute only.
A program may use at most 192 MiB of HBM per device.

v0:
```python
import math

import jax
import jax.numpy as jnp
from jax import lax
from jax.sharding import PartitionSpec as P

RADIX = 32


def passed_along(value, axis, steps):
    count = lax.axis_size(axis)
    pairs = [(source, (source + steps) % count) for source in range(count)]
    return lax.ppermute(value, axis, pairs)


def contract(pattern, operand, matrix):
    return jnp.einsum(
        pattern,
        operand,
        matrix,
        precision=lax.Precision.HIGHEST,
        preferred_element_type=jnp.float32,
    )


def angles(count_a, count_b, period):
    left_index = jnp.arange(count_a, dtype=jnp.int32)[:, None]
    right_index = jnp.arange(count_b, dtype=jnp.int32)[None, :]
    reduced = left_index * right_index % period
    return reduced.astype(jnp.float32) * (2.0 * math.pi / period)


def rotate(pattern, real_part, imag_part, cosine, sine_part):
    if imag_part is None:
        return (contract(pattern, real_part, cosine), contract(pattern, real_part, sine_part))
    real_next = contract(pattern, real_part, cosine) - contract(pattern, imag_part, sine_part)
    imag_next = contract(pattern, real_part, sine_part) + contract(pattern, imag_part, cosine)
    return (real_next, imag_next)


def fourier(real_part, imag_part, radix_len, sign_value, middle, real_only):
    axis_pos = real_part.ndim - 2 if middle else real_part.ndim - 1
    length = real_part.shape[axis_pos]
    inner_len = length // radix_len
    lead_shape = real_part.shape[:axis_pos]
    trail_shape = real_part.shape[axis_pos + 1 :]
    split_shape = lead_shape + (radix_len, inner_len) + trail_shape
    whole_shape = lead_shape + (length,) + trail_shape
    real_part = real_part.reshape(split_shape)
    if imag_part is not None:
        imag_part = imag_part.reshape(split_shape)
    first_angle = angles(radix_len, radix_len, radix_len)
    twiddle = angles(radix_len, inner_len, length)
    second = angles(inner_len, inner_len, inner_len)
    if middle:
        form_one = "...abx,ak->...kbx"
        form_two = "...kbx,bm->...mkx"
        twiddle = twiddle[:, :, None]
    else:
        form_one = "...ab,ak->...kb"
        form_two = "...kb,bm->...mk"
    real_part, imag_part = rotate(
        form_one, real_part, imag_part, jnp.cos(first_angle), sign_value * jnp.sin(first_angle)
    )
    cosine = jnp.cos(twiddle)
    sine_part = sign_value * jnp.sin(twiddle)
    real_part, imag_part = (
        real_part * cosine - imag_part * sine_part,
        real_part * sine_part + imag_part * cosine,
    )
    cosine_two = jnp.cos(second)
    sine_two = sign_value * jnp.sin(second)
    if real_only:
        result = contract(form_two, real_part, cosine_two) - contract(form_two, imag_part, sine_two)
        return (result.reshape(whole_shape), None)
    real_part, imag_part = rotate(form_two, real_part, imag_part, cosine_two, sine_two)
    return (real_part.reshape(whole_shape), imag_part.reshape(whole_shape))


def harmonic(first_cell, second_cell):
    return 2.0 * first_cell * second_cell / (first_cell + second_cell)


def shards(white_noise, amplitude, offsets):
    layers, tile_rows, tile_width = white_noise.shape
    full_height = tile_rows * lax.axis_size("gy")
    real_part, imag_part = fourier(white_noise, None, RADIX, -1.0, False, False)
    arrived = lax.all_to_all(
        jnp.stack([real_part, imag_part]), "gy", split_axis=3, concat_axis=2, tiled=True
    )
    real_part, imag_part = fourier(arrived[0], arrived[1], RADIX, -1.0, True, False)
    real_part, imag_part = fourier(
        real_part * amplitude, imag_part * amplitude, RADIX, 1.0, True, False
    )
    arrived = lax.all_to_all(
        jnp.stack([real_part, imag_part]), "gy", split_axis=2, concat_axis=3, tiled=True
    )
    log_field, unused = fourier(arrived[0], arrived[1], RADIX, 1.0, False, True)
    log_field = log_field * (1.0 / (tile_width * full_height))
    permeability = jnp.exp(log_field)
    trans_x = harmonic(permeability, jnp.roll(permeability, -1, axis=2))
    shift_y = offsets[0]
    shift_x = offsets[1]
    column_sums = jnp.stack([jnp.sum(permeability, axis=0), jnp.sum(1.0 / permeability, axis=0)])
    across = (
        jnp.roll(column_sums, -shift_x, axis=2)
        .reshape(2, tile_rows, tile_width // 8, 8)
        .sum(axis=3)
    )
    rolled = jnp.roll(across, -shift_y, axis=1)
    tail_rows = (jnp.arange(tile_rows, dtype=jnp.int32) >= tile_rows - shift_y)[None, :, None]
    kept_rows = jnp.where(tail_rows, 0.0, rolled)
    lead_sums = jnp.sum(jnp.where(tail_rows, rolled, 0.0), axis=1)
    upper_row, upper_lead = passed_along((permeability[:, 0, :], lead_sums), "gy", -1)
    south_cell = jnp.concatenate([permeability[:, 1:, :], upper_row[:, None, :]], axis=1)
    trans_y = harmonic(permeability, south_cell)
    blocks = kept_rows.reshape(2, tile_rows // 8, 8, tile_width // 8).sum(axis=2)
    blocks = blocks.at[:, -1, :].add(upper_lead)
    totals = lax.psum_scatter(blocks, "gx", scatter_dimension=2, tiled=True)
    upscaled = jnp.sqrt(totals[0] / totals[1])
    return (trans_x, trans_y, upscaled)


def solution(mesh):
    return jax.shard_map(
        shards,
        mesh=mesh,
        in_specs=(P("gx", "gy", None), P(None, "gy"), P()),
        out_specs=(P("gx", "gy", None), P("gx", "gy", None), P("gy", "gx")),
        check_vma=False,
    )
```

profile of v0, /device:TPU:0, one launch (start us, length us, event | category | flops | bytes accessed | tf_op | source)
XLA Modules:
  0.0 1521.5 jit_solution(10151205767198643150)
XLA Ops:
  12.5 9.6 fusion.136
  22.1 13.1 fusion.10
  35.2 13.6 fusion.51
  48.7 13.3 fusion.49
  62.0 15.9 %subtract_bitcast_fusion = f32[1,512,128,32]{1,2,3,0:T(8,128)} fusion(f32[128,512,32]{1,0,2:T(8,128)} %fusion.51, f32[512,32,128]{2,1,0:T(8,128)S(1)} %get-tuple-element.33), kind=kOutput, calls=%fused_computation.43 | convolution fusion | flops 3223552000 | bytes 25165824 | tf_op jit(solution)/shard_map/...kb,bm->...mk/dot_general | solution.py:18
  77.9 11.7 copy.144
  89.6 13.7 add_bitcast_fusion
  103.3 11.8 copy.147
  120.0 31.6 %copy.148 = f32[2,1,512,4096]{2,1,0,3:T(1,128)} copy(f32[2,1,512,4096]{2,3,1,0:T(8,128)S(1)} %pad_maximum_fusion) | data formatting | bytes 33554432 | tf_op jit(solution)/shard_map/stack | solution.py:90
  158.3 363.5 %all-to-all-done = f32[2,1,512,4096]{2,1,0,3:T(1,128)} async-done(((f32[2,1,512,4096]{2,1,0,3:T(1,128)}), f32[2,1,512,4096]{2,1,0,3:T(1,128)}, u32[]{:S(2)}, u32[]{:S(2)}) %all-to-all-start) | async-done | bytes 16777248 | tf_op jit(solution)/shard_map/all_to_all | solution.py:89
  536.9 9.2 copy.152
  546.0 17.3 %fusion.41 = f32[32,128,512]{2,0,1:T(8,128)} fusion(f32[32,128,512]{2,1,0:T(8,128)} %bitcast.198), kind=kOutput, calls=%fused_computation.68 | convolution fusion | flops 805320704 | bytes 16777216 | tf_op jit(solution)/shard_map/...abx,ak->...kbx/dot_general | solution.py:18
  563.3 13.3 fusion.43
  576.6 9.2 copy.150
  585.7 17.6 %fusion.47 = f32[32,128,512]{2,0,1:T(8,128)} fusion(f32[32,128,512]{2,1,0:T(8,128)} %bitcast.200), kind=kOutput, calls=%fused_computation.74 | convolution fusion | flops 805320704 | bytes 16777216 | tf_op jit(solution)/shard_map/...abx,ak->...kbx/dot_general | solution.py:18
  603.3 24.4 %multiply_subtract_fusion.1 = (f32[32,128,512]{2,0,1:T(8,128)}, f32[32,128,512]{2,0,1:T(8,128)}) fusion(f32[32,128]{0,1:T(8,128)S(1)} %copy.157, f32[32,128]{0,1:T(8,128)S(1)} %copy.154, f32[32,128,512]{2,0,1:T(8,128)} %fusion.41, f32[32,128,512]{2,0,1:T(8,128)} %fusion.47, f32[32,128,512]{2,0,1:T(8,128)} %fusion.43, f32[32,128,512]{2,1,0:T(8,128)} %bitcast.201), kind=kOutput, calls=%fused_computation.41 | convolution fusion | flops 822098944 | bytes 50364416 | tf_op jit(solution)/shard_map/...abx,ak->...kbx/dot_general | solution.py:18
  627.7 18.3 %fusion.35 = f32[128,32,512]{2,0,1:T(8,128)} fusion(f32[32,128,512]{2,0,1:T(8,128)} %get-tuple-element.30), kind=kOutput, calls=%fused_computation.62 | convolution fusion | flops 3221471232 | bytes 16777216 | tf_op jit(solution)/shard_map/...kbx,bm->...mkx/dot_general | solution.py:18
  646.0 12.4 fusion.33
  658.4 15.5 %fusion.61 = f32[128,32,512]{2,0,1:T(8,128)} fusion(f32[128,32,512]{2,0,1:T(8,128)} %fusion.35, f32[32,128,512]{2,0,1:T(8,128)S(1)} %bitcast.189), kind=kOutput, calls=%fused_computation.87 | convolution fusion | flops 3223552000 | bytes 25165824 | tf_op jit(solution)/shard_map/...kbx,bm->...mkx/dot_general | solution.py:18
  673.9 11.5 copy.160
  685.4 13.7 fusion.64
  699.1 11.6 copy.164
  710.7 13.7 bitcast_multiply_fusion.4
  724.5 13.1 fusion.25
  737.6 13.3 fusion.27
  750.9 13.1 fusion.31
  764.0 24.5 %multiply_subtract_fusion = (f32[32,128,512]{2,0,1:T(8,128)}, f32[32,128,512]{2,0,1:T(8,128)}) fusion(f32[32,128]{0,1:T(8,128)S(1)} %copy.168, f32[32,128]{0,1:T(8,128)S(1)} %copy.154, f32[32,128,512]{2,0,1:T(8,128)} %fusion.25, f32[32,128,512]{2,0,1:T(8,128)} %fusion.31, f32[32,128,512]{2,0,1:T(8,128)} %fusion.27, f32[32,128,512]{2,1,0:T(8,128)} %bitcast.194), kind=kOutput, calls=%fused_computation.39 | convolution fusion | flops 822097920 | bytes 50364416 | tf_op jit(solution)/shard_map/...abx,ak->...kbx/dot_general | solution.py:18
  788.6 17.7 %fusion.19 = f32[128,32,512]{2,0,1:T(8,128)} fusion(f32[32,128,512]{2,0,1:T(8,128)} %get-tuple-element.28), kind=kOutput, calls=%fused_computation.46 | convolution fusion | flops 3221454848 | bytes 16777216 | tf_op jit(solution)/shard_map/...kbx,bm->...mkx/dot_general | solution.py:18
  806.3 12.4 fusion.17
  818.7 15.5 %fusion.67 = f32[128,32,512]{2,0,1:T(8,128)} fusion(f32[128,32,512]{2,0,1:T(8,128)} %fusion.19, f32[32,128,512]{2,0,1:T(8,128)S(1)} %bitcast.187), kind=kOutput, calls=%fused_computation.89 | convolution fusion | flops 3223552000 | bytes 25165824 | tf_op jit(solution)/shard_map/...kbx,bm->...mkx/dot_general | solution.py:18
  834.3 11.5 copy.171
  845.8 13.9 fusion.70
  859.7 11.8 copy.174
  876.4 31.4 %copy.175 = f32[2,1,4096,512]{3,1,0,2:T(1,128)} copy(f32[2,1,4096,512]{3,2,1,0:T(8,128)S(1)} %pad_maximum_fusion.1) | data formatting | bytes 33554432 | tf_op jit(solution)/shard_map/stack | solution.py:97
  914.9 362.4 %all-to-all-done.1 = f32[2,1,4096,512]{3,1,0,2:T(1,128)} async-done(((f32[2,1,4096,512]{3,1,0,2:T(1,128)}), f32[2,1,4096,512]{3,1,0,2:T(1,128)}, u32[]{:S(2)}, u32[]{:S(2)}) %all-to-all-start.1) | async-done | bytes 16777248 | tf_op jit(solution)/shard_map/all_to_all | solution.py:96
  1292.6 11.5 copy.178
  1304.1 8.9 reshape.524
  1313.0 12.6 fusion.130
  1325.6 9.7 fusion.138
  1343.6 8.9 reshape.523
  1352.5 12.1 fusion.128
  1364.6 18.8 %fusion.6 = (f32[512,32,128]{2,1,0:T(8,128)}, f32[512,32,128]{2,1,0:T(8,128)}) fusion(f32[32,128]{1,0:T(8,128)S(1)} %copy-done.14, f32[32,128]{1,0:T(8,128)S(1)} %copy-done.12, f32[32,512,128]{2,0,1:T(8,128)} %fusion.128, f32[32,512,128]{2,0,1:T(8,128)} %fusion.138, f32[32,512,128]{2,0,1:T(8,128)} %fusion.130, f32[512,32,128]{2,1,0:T(8,128)} %reshape.523), kind=kOutput, calls=%fused_computation.16 | convolution fusion | flops 822097920 | bytes 50364416 | tf_op jit(solution)/shard_map/...ab,ak->...kb/dot_general | solution.py:18
  1383.4 17.4 %fusion.13 = f32[128,512,32]{1,0,2:T(8,128)S(1)} fusion(f32[512,32,128]{2,1,0:T(8,128)} %get-tuple-element.32), kind=kOutput, calls=%fused_computation.31 | convolution fusion | flops 3221454848 | bytes 16777216 | tf_op jit(solution)/shard_map/...kb,bm->...mk/dot_general | solution.py:18
  1400.8 20.3 %exponential_bitcast_fusion = f32[1,512,128,32]{1,2,3,0:T(8,128)S(1)} fusion(f32[128,512,32]{1,0,2:T(8,128)S(1)} %fusion.13, f32[512,32,128]{2,1,0:T(8,128)} %get-tuple-element.31), kind=kOutput, calls=%fused_computation.37 | convolution fusion | flops 3225649152 | bytes 25165824 | tf_op jit(solution)/shard_map/...kb,bm->...mk/dot_general | solution.py:18
  1447.6 17.8 %broadcast_divide_fusion = (f32[1,512,4096]{1,2,0:T(8,128)S(1)}, f32[1,512,4096]{1,2,0:T(8,128)}, f32[1,512,4096]{1,2,0:T(8,128)}) fusion(f32[1,512,128,32]{1,3,2,0:T(8,128)} %copy-done, f32[1,512,1]{1,2,0:T(1,128)S(1)} %slice.82, f32[1,512,4095]{1,2,0:T(8,128)} %slice.81, f32[1,1,4096]{1,2,0:T(8,128)S(1)} %copy.182, f32[1,511,4096]{1,2,0:T(8,128)} %slice.83), kind=kLoop, calls=%fused_computation.86 | loop fusion | flops 20971520 | bytes 50331648 | tf_op jit(solution)/shard_map/div | solution.py:105
  1465.5 13.0 fusion.3
  1486.6 8.9 copy.184
  1495.5 8.9 copy.185
  (88 shorter events, 108.9 us)
Async XLA Ops:
  7.3 150.6 %copy-start.11 = (f32[32,128]{1,0:T(8,128)}, f32[32,128]{1,0:T(8,128)S(1)}, u32[]{:S(2)}) copy-start(f32[32,128]{1,0:T(8,128)S(1)} %get-tuple-element.49) | copy-start | bytes 49156
  12.5 9.6 copy-start.2
  77.9 11.7 copy-start.7
  103.3 11.8 copy-start.8
  151.6 370.2 %all-to-all-start = ((f32[2,1,512,4096]{2,1,0,3:T(1,128)}), f32[2,1,512,4096]{2,1,0,3:T(1,128)}, u32[]{:S(2)}, u32[]{:S(2)}) async-start(f32[2,1,512,4096]{2,1,0,3:T(1,128)} %copy.148), calls=%async_computation | async-start | bytes 33554432 | tf_op jit(solution)/shard_map/all_to_all | solution.py:89
  158.2 371.7 %copy-start.13 = (f32[32,128]{1,0:T(8,128)}, f32[32,128]{1,0:T(8,128)S(1)}, u32[]{:S(2)}) copy-start(f32[32,128]{1,0:T(8,128)S(1)} %fusion.160) | copy-start | bytes 49156
  546.0 17.3 %copy-start.3 = (f32[1,1,8,512,512]{4,3,2,1,0:T(8,128)S(1)}, f32[1,1,8,512,512]{4,3,2,1,0:T(8,128)}, u32[]{:S(2)}) copy-start(f32[1,1,8,512,512]{4,3,2,1,0:T(8,128)} %copy.152) | copy-start | bytes 25165828
  627.7 18.3 %copy-start.6 = (f32[32,128,512]{2,0,1:T(8,128)S(1)}, f32[32,128,512]{2,0,1:T(8,128)}, u32[]{:S(2)}) copy-start(f32[32,128,512]{2,0,1:T(8,128)} %get-tuple-element.30) | copy-start | bytes 25165828
  627.7 30.7 %slice-start.2 = ((s8[8388608]{0:T(1024)(128)(4,1)}), s8[4194304]{0:T(1024)(128)(4,1)S(1)}, s32[]{:S(2)}) async-start(s8[8388608]{0:T(1024)(128)(4,1)} %bitcast.188), calls=%async_computation.6 | async-start | bytes 8388608
  646.0 12.4 slice-start.3
  724.5 26.5 %slice-start.4 = ((s8[8388608]{0:T(1024)(128)(4,1)}), s8[4194304]{0:T(1024)(128)(4,1)S(1)}, s32[]{:S(2)}) async-start(s8[8388608]{0:T(1024)(128)(4,1)} %bitcast.195), calls=%async_computation.8 | async-start | bytes 8388608
  737.6 13.3 slice-start.5
  788.6 17.7 %copy-start.5 = (f32[32,128,512]{2,0,1:T(8,128)S(1)}, f32[32,128,512]{2,0,1:T(8,128)}, u32[]{:S(2)}) copy-start(f32[32,128,512]{2,0,1:T(8,128)} %get-tuple-element.28) | copy-start | bytes 25165828
  788.6 30.1 %slice-start = ((s8[8388608]{0:T(1024)(128)(4,1)}), s8[4194304]{0:T(1024)(128)(4,1)S(1)}, s32[]{:S(2)}) async-start(s8[8388608]{0:T(1024)(128)(4,1)} %bitcast.186), calls=%async_computation.4 | async-start | bytes 8388608
  806.3 12.4 slice-start.1
  859.7 11.8 copy-start.9
  907.8 6.0 copy-start.15
  907.8 369.6 %all-to-all-start.1 = ((f32[2,1,4096,512]{3,1,0,2:T(1,128)}), f32[2,1,4096,512]{3,1,0,2:T(1,128)}, u32[]{:S(2)}, u32[]{:S(2)}) async-start(f32[2,1,4096,512]{3,1,0,2:T(1,128)} %copy.175), calls=%async_computation.1 | async-start | bytes 33554432 | tf_op jit(solution)/shard_map/all_to_all | solution.py:96
  913.7 599.1 %reduce-scatter.2.cloned.1.call-start = ((), (), s32[]{:S(2)}) async-start(), calls=%async_computation.3 | async-start | bytes 327680 | tf_op jit(solution)/shard_map/reduce_scatter | solution.py:120
  1313.0 12.6 copy-start.4
  1313.0 22.3 %slice-start.6 = ((s8[8388608]{0:T(1024)(128)(4,1)}), s8[4194304]{0:T(1024)(128)(4,1)S(1)}, s32[]{:S(2)}) async-start(s8[8388608]{0:T(1024)(128)(4,1)} %bitcast.204), calls=%async_computation.10 | async-start | bytes 8388608
  1325.6 9.7 slice-start.7
  1352.5 12.1 copy-start.12
  1352.5 12.1 copy-start.14
  1426.0 3.4 copy-start
  1430.0 17.0 %collective-permute-start = (f32[1,4096]{1,0:T(1,128)S(1)}, f32[1,4096]{1,0:T(1,128)S(1)}, u32[]{:S(2)}, u32[]{:S(2)}) collective-permute-start(f32[1,4096]{1,0:T(1,128)S(1)} %bitcast.212), channel_id=1, source_target_pairs={{0,7},{1,0},{2,1},{3,2},{4,3},{5,4},{6,5},{7,6},{8,15},{9,8},{10,9... | collective-permute-start | bytes 49160 | tf_op jit(solution)/shard_map/ppermute | solution.py:14
  1433.4 8.1 copy-start.1
  1484.0 1.8 collective-permute-start.1
  1485.9 0.7 copy-start.10
Sparse Core Ops, SparseCore 0:
  1486.8 25.9 reduce-scatter.1
where the time goes:
time: 1530 us; the launch traced here: 1520 us
  waiting for transfers between devices  735 us (48%)
  matrix products  426 us (28%)
  local copies, waits for them, and re-layouts  269 us (18%)
  other arithmetic  60.2 us (4%)
  between operations  17.9 us (1%)
    dot_general x28, matrix products, contract(): jnp.einsum(pattern, operand, matrix, precision=lax.Precision.HIGHEST, pre...  426 us
    all_to_all x1, waiting for transfers between devices, shards(): lax.all_to_all(jnp.stack([real_part, imag_part]), 'gy', split_axis=3, con...  363 us
    all_to_all x1, waiting for transfers between devices, shards(): lax.all_to_all(jnp.stack([real_part, imag_part]), 'gy', split_axis=2, con...  362 us
    another operation x2, local copies, waits for them, and re-layouts, shards(): jnp.stack([real_part, imag_part])  62.9 us
    add x3, local copies, waits for them, and re-layouts, rotate(): contract(pattern, real_part, sine_part)  35.2 us
    sub x3, local copies, waits for them, and re-layouts, rotate(): contract(pattern, real_part, cosine)  34.7 us
  transfers between devices with their start and end apart: 5, of which 4 were waited for; matrix products, arithmetic and copies ran while one was open for 2% of the time, Pallas kernels for 0%

commit v1 on v0

v1 whole, which is shorter than its diff:
```python
import functools
import math

import jax
import jax.numpy as jnp
import ml_dtypes
import numpy as np
from jax import lax
from jax.experimental import pallas as pl
from jax.experimental.pallas import tpu as pltpu
from jax.sharding import PartitionSpec as P

LANES = 128
RADIX = 32
GROUPS = RADIX // 2
LENGTH = RADIX * LANES
PAIR = 2 * LANES
BLOCK = 8
VMEM_BYTES = 56 * 1024 * 1024

CLASSES = [(0, RADIX // 2)] + [(k, RADIX - k) for k in range(1, GROUPS)]


def pair_matrices():
    lane = np.arange(LANES)[None, :]
    place = np.arange(LANES)[:, None]
    matrices = np.zeros((GROUPS, PAIR, PAIR), np.float64)
    for group, classes in enumerate(CLASSES):
        for half, class_index in enumerate(classes):
            angle = 2.0 * math.pi * (lane * (class_index + RADIX * place) % LENGTH) / LENGTH
            both = np.cos(angle) + np.sin(angle)
            turned = np.sin(angle) - np.cos(angle)
            rows = slice(half * LANES, (half + 1) * LANES)
            if group == 0:
                matrices[0, rows, rows] = both
            else:
                matrices[group, rows, :LANES] = both
                matrices[group, rows, LANES:] = turned if half == 0 else -turned
    return matrices


def two_parts(matrices):
    high = matrices.astype(ml_dtypes.bfloat16)
    low = (matrices - high.astype(np.float64)).astype(ml_dtypes.bfloat16)
    return np.stack([high, low])


@functools.cache
def tables():
    ahead = pair_matrices()
    scale = np.full((GROUPS, 1, 1), 1.0 / (2 * LANES * RADIX))
    scale[0] = 1.0 / (LANES * RADIX)
    back = ahead * scale
    return two_parts(ahead), two_parts(np.swapaxes(ahead, 1, 2)), two_parts(back)


def spread(values):
    count = len(values)
    if count == 1:
        return [values[0]], [None]
    if count == 2:
        return [values[0] + values[1], values[0] - values[1]], [None, None]
    quarter, half = count // 4, count // 2
    even_re, even_im = spread(values[0::2])
    odd_re, odd_im = spread(values[1::2])
    out_re, out_im = [None] * (half + 1), [None] * (half + 1)
    out_re[0] = even_re[0] + odd_re[0]
    out_re[half] = even_re[0] - odd_re[0]
    out_re[quarter] = even_re[quarter]
    out_im[quarter] = -odd_re[quarter]
    for k in range(1, quarter):
        cosine, sine = math.cos(2 * math.pi * k / count), math.sin(2 * math.pi * k / count)
        turned_re = cosine * odd_re[k] + sine * odd_im[k]
        turned_im = cosine * odd_im[k] - sine * odd_re[k]
        out_re[k] = even_re[k] + turned_re
        out_im[k] = even_im[k] + turned_im
        out_re[half - k] = even_re[k] - turned_re
        out_im[half - k] = turned_im - even_im[k]
    return out_re, out_im


def gather(real, imag):
    half = len(real) - 1
    if half == 0:
        return [real[0]]
    if half == 1:
        return [real[0] + real[1], real[0] - real[1]]
    count, quarter = 2 * half, half // 2
    even_re, even_im = [None] * (quarter + 1), [None] * (quarter + 1)
    odd_re, odd_im = [None] * (quarter + 1), [None] * (quarter + 1)
    even_re[0] = real[0] + real[half]
    odd_re[0] = real[0] - real[half]
    even_re[quarter] = real[quarter] + real[quarter]
    odd_re[quarter] = -(imag[quarter] + imag[quarter])
    for k in range(1, quarter):
        cosine, sine = math.cos(2 * math.pi * k / count), math.sin(2 * math.pi * k / count)
        even_re[k] = real[k] + real[half - k]
        even_im[k] = imag[k] - imag[half - k]
        diff_re = real[k] - real[half - k]
        diff_im = imag[k] + imag[half - k]
        odd_re[k] = cosine * diff_re - sine * diff_im
        odd_im[k] = sine * diff_re + cosine * diff_im
    values = [None] * count
    values[0::2] = gather(even_re, even_im)
    values[1::2] = gather(odd_re, odd_im)
    return values


def store_groups(ref, at, values):
    real, imag = spread(values)
    for group in range(GROUPS):
        ref[group, at, :LANES] = real[group]
        ref[group, at, LANES:] = imag[group] if group else real[GROUPS]


def load_groups(ref, at):
    pairs = [(ref[group, at, :LANES], ref[group, at, LANES:]) for group in range(GROUPS)]
    real = [pair[0] for pair in pairs] + [pairs[0][1]]
    imag = [None] + [pair[1] for pair in pairs[1:]] + [None]
    return gather(real, imag)


def halves(value):
    high = value.astype(jnp.bfloat16)
    return high, (value - high.astype(jnp.float32)).astype(jnp.bfloat16)


def dot(left, right, right_axis=0):
    return lax.dot_general(
        left, right, (((1,), (right_axis,)), ((), ())), preferred_element_type=jnp.float32
    )


def times_table(value, table_ref, group):
    high, low = halves(value)
    return dot(high, table_ref[0, group]) + (
        dot(low, table_ref[0, group]) + dot(high, table_ref[1, group])
    )


def strip_at(index):
    return pl.ds(pl.multiple_of(index * BLOCK, BLOCK), BLOCK)


def lanes_of(index):
    return slice(index * LANES, (index + 1) * LANES)


def taken(refs, kinds, count):
    chunks = []
    for stacked in kinds:
        held = 1 if stacked else count
        chunks.append(list(refs[:held]))
        refs = refs[held:]
    return chunks, refs


def view(chunk, stacked, me, step):
    if stacked:
        return step, chunk[0].at[step]
    return me ^ step, chunk[step]


def forward_x(count, cuts, kinds, me_ref, noise_ref, table_ref, *refs):
    outs, (group_ref, spectrum_ref) = taken(refs, kinds, count)
    rows = noise_ref.shape[1]
    share = LANES // count
    me = me_ref[0]

    def strip(index, carry):
        at = strip_at(index)
        store_groups(group_ref, at, [noise_ref[0, at, lanes_of(a)] for a in range(RADIX)])
        return carry

    lax.fori_loop(0, rows // BLOCK, strip, 0, unroll=2)
    for cut, (first, last) in enumerate(cuts):

        def group_step(group, carry, cut=cut, first=first):
            high, low = halves(group_ref[group])
            both = dot(table_ref[0, group], jnp.concatenate([high, low], axis=0), 1)
            spectrum_ref[...] = (both[:, :rows] + both[:, rows:]) + dot(table_ref[1, group], high, 1)
            for step in range(count):
                place, out = view(outs[cut], kinds[cut], me, step)
                for half in range(2):
                    source = pl.multiple_of(half * LANES + place * share, share)
                    target = pl.multiple_of(((group - first) * 2 + half) * share, share)
                    out[pl.ds(target, share), :] = spectrum_ref[pl.ds(source, share), :]
            return carry

        lax.fori_loop(first, last, group_step, 0, unroll=4)


def filter_y(count, in_cuts, in_kinds, out_cuts, out_kinds, gains, me_ref, *refs):
    ins, refs = taken(refs, in_kinds, count)
    gain_refs, (ahead_ref, back_ref) = refs[:gains], refs[gains : gains + 2]
    outs, (field_ref, group_ref) = taken(refs[gains + 2 :], out_kinds, count)
    rows = field_ref.shape[1]
    per = field_ref.shape[2] // LANES
    me = me_ref[0]
    for chunk, stacked, (first, last) in zip(ins, in_kinds, in_cuts):
        for step in range(count):
            place, piece = view(chunk, stacked, me, step)
            field_ref[place, :, first:last] = piece[...]

    def ahead_strip(index, carry):
        at = strip_at(index)
        values = [field_ref[a // per, at, lanes_of(a % per)] for a in range(RADIX)]
        store_groups(group_ref, at, values)
        return carry

    lax.fori_loop(0, rows // BLOCK, ahead_strip, 0, unroll=2)

    def group_step(group, carry):
        spectrum = times_table(group_ref[group], ahead_ref, group)
        other = jnp.where(group == 0, RADIX // 2, RADIX - group)
        columns = [
            pl.ds(pl.multiple_of(place * LANES, LANES), LANES) for place in (group, other)
        ]
        gain = jnp.concatenate(
            [
                jnp.concatenate([ref[0, :, column] for ref in gain_refs], axis=0)
                for column in columns
            ],
            axis=1,
        )
        group_ref[group] = times_table(spectrum * gain, back_ref, group)
        return carry

    lax.fori_loop(0, GROUPS, group_step, 0, unroll=4)

    def back_strip(index, carry):
        at = strip_at(index)
        for a, value in enumerate(load_groups(group_ref, at)):
            field_ref[a // per, at, lanes_of(a % per)] = value
        return carry

    lax.fori_loop(0, rows // BLOCK, back_strip, 0, unroll=2)
    for chunk, stacked, (first, last) in zip(outs, out_kinds, out_cuts):
        for step in range(count):
            place, piece = view(chunk, stacked, me, step)
            piece[...] = field_ref[place, :, first:last]


def inverse_x(
    count, cuts, kinds, layer, start, has_before, has_after, aliased, me_ref, offsets_ref, *refs
):
    ins, refs = taken(refs, kinds, count)
    table_ref, refs = refs[0], refs[1:]
    before_ref = after_ref = None
    if has_before:
        before_ref, refs = refs[0], refs[1:]
    if has_after:
        after_ref, refs = refs[0], refs[1:]
    if aliased:
        refs = refs[2:]
    face_x_hbm, face_y_hbm, sums_ref, first_ref, last_ref, *scratch = refs
    piece_ref, group_ref, upper_ref, lower_ref, face_x, face_y, column_ref, sems = scratch
    rows = face_x.shape[0]
    tiles = rows // BLOCK
    share = LANES // count
    me = me_ref[0]
    lead = 1 if has_before else 0
    made = tiles - 1 + lead + (1 if has_after else 0)
    width = RADIX * LANES

    for chunk, stacked, (first, last) in zip(ins, kinds, cuts):
        span = slice(2 * share * first, 2 * share * last)
        for step in range(count):
            place, piece = view(chunk, stacked, me, step)
            piece_ref[place, span, :] = piece[...]

    def group_step(group, carry):
        parts = []
        for half in range(2):
            at = pl.ds(pl.multiple_of((2 * group + half) * share, share), share)
            parts.append(piece_ref[:, at, :].reshape(LANES, rows))
        stacked = jnp.concatenate(parts, axis=0)
        group_ref[group] = times_table(stacked.T, table_ref, group)
        return carry

    lax.fori_loop(0, GROUPS, group_step, 0, unroll=4)

    def raised(field, at, a):
        upper_ref[at, lanes_of(a)] = jnp.exp(field)
        lower_ref[at, lanes_of(a)] = jnp.exp(-field)

    def field_strip(index, carry, copy_ref=None):
        at = strip_at(index)
        to = strip_at(index + lead)
        for a, value in enumerate(load_groups(group_ref, at)):
            raised(value, to, a)
            if copy_ref is not None:
                copy_ref[:, lanes_of(a)] = value
        return carry

    field_strip(0, 0, first_ref)
    lax.fori_loop(1, tiles - 1, field_strip, 0, unroll=2)
    field_strip(tiles - 1, 0, last_ref)
    for a in range(RADIX):
        if has_before:
            raised(before_ref[:, lanes_of(a)], slice(0, BLOCK), a)
        if has_after:
            end = (lead + tiles) * BLOCK
            raised(after_ref[:, lanes_of(a)], slice(end, end + BLOCK), a)

    row_index = lax.broadcasted_iota(jnp.int32, (BLOCK, LANES), 0)
    lane_index = lax.broadcasted_iota(jnp.int32, (BLOCK, LANES), 1)
    own_rows = row_index >= offsets_ref[0]
    last_row = row_index == BLOCK - 1
    last_lane = lane_index == LANES - 1

    def x_strip(index, carry):
        at = strip_at(index)
        here = [lower_ref[strip_at(index + lead), lanes_of(a)] for a in range(RADIX)]
        moved = [pltpu.roll(value, LANES - 1, 1) for value in here]
        for a in range(RADIX):
            beside = jnp.where(last_lane, moved[(a + 1) % RADIX], moved[a])
            face_x[at, lanes_of(a)] = 2.0 / (here[a] + beside)
        return carry

    lax.fori_loop(0, tiles, x_strip, 0, unroll=2)
    copy_x = pltpu.make_async_copy(
        face_x, face_x_hbm.at[layer, pl.ds(start, rows), :], sems.at[0]
    )
    copy_x.start()

    def add_row(kind, index, a, value):
        at = strip_at(index // BLOCK)
        total = jnp.sum(value, axis=0, keepdims=True)
        column_ref[kind, at, lanes_of(a)] = jnp.where(
            row_index == index % BLOCK, total, column_ref[kind, at, lanes_of(a)]
        )

    def y_strip(index, carry):
        at = strip_at(index)
        then = strip_at(index + 1)
        for a in range(RADIX):
            here, below = lower_ref[at, lanes_of(a)], lower_ref[then, lanes_of(a)]
            moved = pltpu.roll(jnp.where(row_index == 0, below, here), BLOCK - 1, 0)
            face_y[at, lanes_of(a)] = 2.0 / (here + moved)
            add_row(1, index, a, jnp.where(own_rows, here, below))
            here, below = upper_ref[at, lanes_of(a)], upper_ref[then, lanes_of(a)]
            add_row(0, index, a, jnp.where(own_rows, here, below))
        return carry

    lax.fori_loop(0, made, y_strip, 0, unroll=2)
    copy_y = pltpu.make_async_copy(
        face_y, face_y_hbm.at[layer, pl.ds(start - BLOCK * lead, made * BLOCK), :], sems.at[1]
    )
    copy_y.start()

    column_ref[:, :, width:] = column_ref[:, :, :LANES]
    reach = BLOCK * LANES + LANES
    lane = lax.broadcasted_iota(jnp.int32, (reach, LANES), 0)
    block = lax.broadcasted_iota(jnp.int32, (reach, LANES), 1)
    inside = lane - offsets_ref[1] - BLOCK * block
    chosen = jnp.where((inside >= 0) & (inside < BLOCK), 1.0, 0.0).astype(jnp.bfloat16)
    for kind in range(2):
        for part in range(width // (BLOCK * LANES)):
            at = BLOCK * LANES * part
            high, low = halves(column_ref[kind, :, at : at + reach])
            sums_ref[kind, :, lanes_of(part)] = dot(high, chosen) + dot(low, chosen)
    copy_x.wait()
    copy_y.wait()


def exchange(chunk, axis):
    if not isinstance(chunk, list):
        return lax.all_to_all(chunk, axis, 0, 0, tiled=True)
    count = len(chunk)
    arrived = [chunk[0]] + [None] * (count - 1)
    for step in reversed(range(1, count)):
        pairs = [(device, device ^ step) for device in range(count)]
        arrived[step] = lax.ppermute(chunk[step], axis, pairs)
    return arrived


def flat(chunks):
    return [ref for chunk in chunks for ref in (chunk if isinstance(chunk, list) else [chunk])]


def chunked(refs, kinds, count):
    chunks, _ = taken(refs, kinds, count)
    return [chunk[0] if stacked else chunk for chunk, stacked in zip(chunks, kinds)]


def kinds_of(chunks):
    return [not isinstance(chunk, list) for chunk in chunks]


def block_specs(kinds, count, shapes, place_of):
    specs = []
    for number, (stacked, shape) in enumerate(zip(kinds, shapes)):
        place = place_of(number)
        if stacked:
            specs.append(pl.BlockSpec((count, *shape), lambda i, place=place: (0, *place(i))))
        else:
            specs += [pl.BlockSpec(shape, place)] * count
    return specs


def whole_shapes(kinds, count, shapes):
    made = []
    for stacked, shape in zip(kinds, shapes):
        if stacked:
            made.append(jax.ShapeDtypeStruct((count, *shape), jnp.float32))
        else:
            made += [jax.ShapeDtypeStruct(shape, jnp.float32)] * count
    return made


def scalars():
    return pl.BlockSpec(memory_space=pltpu.SMEM)


def params():
    return pltpu.CompilerParams(vmem_limit_bytes=VMEM_BYTES)


def cost(rows, micros):
    return pl.CostEstimate(
        flops=int(rows * micros * 1.15e9 / 256),
        bytes_accessed=rows * LENGTH * 8,
        transcendentals=0,
    )


def run_forward(me, noise, layer, span, cuts, kinds, count, table):
    share = LANES // count
    first, last = span
    step_rows = LANES
    depths = [2 * share * (end - begin) for begin, end in cuts]
    offset = first // step_rows
    outs = pl.pallas_call(
        functools.partial(forward_x, count, cuts, kinds),
        grid=((last - first) // step_rows,),
        in_specs=[
            scalars(),
            pl.BlockSpec((1, step_rows, LENGTH), lambda i: (layer, i + offset, 0)),
            pl.BlockSpec(table.shape, lambda i: (0, 0, 0, 0), pipeline_mode=pl.Buffered(1)),
        ],
        out_specs=block_specs(
            kinds, count, [(depth, step_rows) for depth in depths], lambda n: lambda i: (0, i)
        ),
        out_shape=whole_shapes(kinds, count, [(depth, last - first) for depth in depths]),
        scratch_shapes=[
            pltpu.VMEM((GROUPS, step_rows, PAIR), jnp.float32),
            pltpu.VMEM((PAIR, step_rows), jnp.float32),
        ],
        compiler_params=params(),
        cost_estimate=cost(last - first, 9),
        name="forward_x",
    )(me, noise, table)
    return chunked(outs, kinds, count)


def run_filter(me, chunks, in_cuts, out_cuts, out_kinds, count, gain, span, ahead, back):
    first_row, rows = span.start, span.stop - span.start
    step_rows = min(rows, LANES)
    lane_count = LENGTH // count
    share = LANES // count
    offset = first_row // step_rows
    in_kinds = kinds_of(chunks)
    skips = [offset if flat([chunk])[0].shape[-2] > rows else 0 for chunk in chunks]
    table_spec = pl.BlockSpec(ahead.shape, lambda i: (0, 0, 0, 0), pipeline_mode=pl.Buffered(1))
    gains = step_rows // share

    def gain_place(number):
        def place(i):
            group = (i + offset) * (gains // 2) + number // 2
            if number % 2 == 0:
                return (group, 0, 0)
            return (jnp.where(group == 0, RADIX // 2, RADIX - group), 0, 0)

        return place

    outs = pl.pallas_call(
        functools.partial(filter_y, count, in_cuts, in_kinds, out_cuts, out_kinds, gains),
        grid=(rows // step_rows,),
        in_specs=[scalars()]
        + block_specs(
            in_kinds,
            count,
            [(step_rows, cut[1] - cut[0]) for cut in in_cuts],
            lambda n: lambda i: (i + skips[n], 0),
        )
        + [pl.BlockSpec((1, share, LENGTH), gain_place(n)) for n in range(gains)]
        + [table_spec, table_spec],
        out_specs=block_specs(
            out_kinds,
            count,
            [(step_rows, cut[1] - cut[0]) for cut in out_cuts],
            lambda n: lambda i: (i, 0),
        ),
        out_shape=whole_shapes(out_kinds, count, [(rows, cut[1] - cut[0]) for cut in out_cuts]),
        scratch_shapes=[
            pltpu.VMEM((count, step_rows, lane_count), jnp.float32),
            pltpu.VMEM((GROUPS, step_rows, PAIR), jnp.float32),
        ],
        compiler_params=params(),
        cost_estimate=cost(rows, 16),
        name="filter_y",
    )(me, *flat(chunks), *[gain] * gains, ahead, back)
    return chunked(outs, out_kinds, count)


def run_inverse(
    me, offsets, chunks, lane_starts, cuts, count, layer, span, table, before, after, faces, shape
):
    first, last = span
    rows = last - first
    tiles = rows // BLOCK
    made = tiles - 1 + (before is not None) + (after is not None)
    padded = -(-made // 16) * 16
    held = tiles + (before is not None) + (after is not None)
    kinds = kinds_of(chunks)
    extra = [value for value in (before, after) if value is not None]
    in_specs = [scalars(), scalars()]
    in_specs += block_specs(
        kinds,
        count,
        [(flat([chunk])[0].shape[-2], rows) for chunk in chunks],
        lambda n: lambda i: (0, lane_starts[n] // rows),
    )
    in_specs += [
        pl.BlockSpec(table.shape, lambda i: (0, 0, 0, 0)),
        *[pl.BlockSpec(value.shape, lambda i: (0, 0)) for value in extra],
    ]
    aliases = {}
    if faces is not None:
        aliases = {len(in_specs): 0, len(in_specs) + 1: 1}
        in_specs += [pl.BlockSpec(memory_space=pl.ANY)] * 2
    face = jax.ShapeDtypeStruct(shape, jnp.float32)
    tile = jax.ShapeDtypeStruct((BLOCK, LENGTH), jnp.float32)
    sums_shape = (2, padded, LENGTH // BLOCK)
    face_x, face_y, sums, first_tile, last_tile = pl.pallas_call(
        functools.partial(
            inverse_x,
            count,
            cuts,
            kinds,
            layer,
            first,
            before is not None,
            after is not None,
            faces is not None,
        ),
        grid=(1,),
        in_specs=in_specs,
        out_specs=[
            pl.BlockSpec(memory_space=pl.ANY),
            pl.BlockSpec(memory_space=pl.ANY),
            pl.BlockSpec(sums_shape, lambda i: (0, 0, 0)),
            pl.BlockSpec(tile.shape, lambda i: (0, 0)),
            pl.BlockSpec(tile.shape, lambda i: (0, 0)),
        ],
        out_shape=[face, face, jax.ShapeDtypeStruct(sums_shape, jnp.float32), tile, tile],
        scratch_shapes=[
            pltpu.VMEM((count, LENGTH // count, rows), jnp.float32),
            pltpu.VMEM((GROUPS, rows, PAIR), jnp.float32),
            pltpu.VMEM((held * BLOCK, LENGTH), jnp.float32),
            pltpu.VMEM((held * BLOCK, LENGTH), jnp.float32),
            pltpu.VMEM((rows, LENGTH), jnp.float32),
            pltpu.VMEM((made * BLOCK, LENGTH), jnp.float32),
            pltpu.VMEM((2, padded, LENGTH + LANES), jnp.float32),
            pltpu.SemaphoreType.DMA((2,)),
        ],
        input_output_aliases=aliases,
        compiler_params=params(),
        cost_estimate=cost(rows, 18),
        name="inverse_x",
    )(me, offsets, *flat(chunks), table, *extra, *(faces or ()))
    return (face_x, face_y), sums[:, :made], first_tile, last_tile


def arranged(amplitude, count):
    share = LANES // count
    table = amplitude.reshape(LANES, RADIX, RADIX * share).transpose(1, 0, 2)
    table = lax.optimization_barrier(table).reshape(LENGTH, RADIX * share).T
    return lax.optimization_barrier(table).reshape(share, RADIX, LENGTH).transpose(1, 0, 2)


def sum_scattered(values, axis):
    count = lax.axis_size(axis)
    me = lax.axis_index(axis)
    width = values.shape[-1] // count
    total = lax.dynamic_slice_in_dim(values, me * width, width, values.ndim - 1)
    for step in range(1, count):
        part = lax.dynamic_slice_in_dim(values, (me ^ step) * width, width, values.ndim - 1)
        total = total + lax.ppermute(part, axis, [(d, d ^ step) for d in range(count)])
    return total


def shards(white_noise, amplitude, offsets):
    layers, rows, _ = white_noise.shape
    count = lax.axis_size("gy")
    share = LANES // count
    me = lax.axis_index("gy").reshape(1)
    analysis, ahead, back = [jnp.asarray(table) for table in tables()]
    arrive_spans = [(0, LANES), (LANES, rows)]
    leave_spans = [(0, rows - LANES), (rows - LANES, rows)]
    done_spans = [(at, min(at + 2 * LANES, rows - LANES)) for at in range(0, rows - LANES, 2 * LANES)]
    done_spans.append((rows - LANES, rows))
    cuts = [(0, GROUPS // 2), (GROUPS // 2, GROUPS)]
    every = [(0, GROUPS)]
    gain = None
    faces = None
    totals = None
    for layer in range(layers):
        (early,) = run_forward(me, white_noise, layer, arrive_spans[0], every, [False], count, analysis)
        early = exchange(early, "gy")
        sent = run_forward(me, white_noise, layer, arrive_spans[1], cuts, [False, False], count, analysis)
        if gain is None:
            amplitude, sent = lax.optimization_barrier((amplitude, sent))
            gain = arranged(amplitude, count)
        late = [exchange(part, "gy") for part in sent]
        returned = []
        for cut, (first, last) in enumerate(cuts):
            span = slice(2 * share * first, 2 * share * last)
            out_cuts, out_kinds = ([(0, rows)], [False]) if cut == 0 else (leave_spans, [False, False])
            made = run_filter(
                me,
                [early, late[cut]],
                arrive_spans,
                out_cuts,
                out_kinds,
                count,
                gain,
                span,
                ahead,
                back,
            )
            returned.append([exchange(part, "gy") for part in made])
        before = after = None
        sums = []
        for index, span in enumerate(done_spans):
            final = index == len(done_spans) - 1
            chunks = [returned[0][0], returned[1][1 if final else 0]]
            lane_starts = [span[0], 0 if final else span[0]]
            if final:
                pairs = [(device, (device - 1) % count) for device in range(count)]
                after = lax.ppermute(first_tile, "gy", pairs)
            faces, part, head, before_next = run_inverse(
                me,
                offsets,
                chunks,
                lane_starts,
                cuts,
                count,
                layer,
                span,
                back,
                before,
                after,
                faces,
                white_noise.shape,
            )
            sums.append(part)
            before = before_next
            if index == 0:
                first_tile = head
        blocks = jnp.concatenate(sums, axis=1)
        totals = blocks if totals is None else totals + blocks
    totals = sum_scattered(totals, "gx")
    return faces[0], faces[1], jnp.sqrt(totals[0] / totals[1])


def solution(mesh):
    return jax.shard_map(
        shards,
        mesh=mesh,
        in_specs=(P("gx", "gy", None), P(None, "gy"), P()),
        out_specs=(P("gx", "gy", None), P("gx", "gy", None), P("gy", "gx")),
        check_vma=False,
    )
```

time: 1530 us -> 425 us (0.28)
  waiting for transfers between devices: 735 us -> 161 us
  matrix products: 426 us -> 0 us
  local copies, waits for them, and re-layouts: 269 us -> 34.9 us
  starting transfers between devices: 13.7 us -> 138 us
  Pallas kernels: 0 us -> 89.2 us
  other arithmetic: 60.2 us -> 0.68 us
  between operations: 17.9 us -> 1.23 us
    all_to_all x2 -> x0, waiting for transfers between devices: 726 us -> none  [the longest x1 363 us: shards(): lax.all_to_all(jnp.stack([real_part, imag_part]), 'gy', split_axis=3, con...]
    dot_general x28 -> x0, matrix products: 426 us -> none  [contract(): jnp.einsum(pattern, operand, matrix, precision=lax.Precision.HIGHEST, pre...]
    ppermute x2 -> x46, waiting for transfers between devices: 0.81 us -> 161 us  [the longest x42 157 us: exchange(): arrived[step] = lax.ppermute(chunk[step], axis, pairs)]
    ppermute x2 -> x46, starting transfers between devices: 1.46 us -> 138 us  [the longest x42 132 us: exchange(): arrived[step] = lax.ppermute(chunk[step], axis, pairs)]
    pallas_call x0 -> x7, Pallas kernels: none -> 89.2 us  [the longest x3 40 us: run_inverse(): pl.pallas_call(functools.partial(inverse_x, count, cuts, kinds, layer, fi...]
    another operation x4 -> x0, local copies, waits for them, and re-layouts: 80.8 us -> none  [the longest x2 62.9 us: shards(): jnp.stack([real_part, imag_part])]
    slice x11 -> x1, local copies, waits for them, and re-layouts: 66.9 us -> 0.9 us  [run_inverse(): return ((face_x, face_y), sums[:, :made], first_tile, last_tile)]
    add x3 -> x0, local copies, waits for them, and re-layouts: 35.2 us -> none  [rotate(): contract(pattern, real_part, sine_part)]
  transfers between devices with their start and end apart: 5 -> 46, of which waited for: 4 -> 14; matrix products, arithmetic and copies ran while one was open for 2% -> 8% of each run, Pallas kernels for 0% -> 17%
where the time goes in v1:
time: 425 us
  waiting for transfers between devices  161 us (38%)
  starting transfers between devices  138 us (32%)
  Pallas kernels  89.2 us (21%)
  local copies, waits for them, and re-layouts  34.9 us (8%)
    ppermute x42, waiting for transfers between devices, exchange(): arrived[step] = lax.ppermute(chunk[step], axis, pairs)  157 us
    ppermute x42, starting transfers between devices, exchange(): arrived[step] = lax.ppermute(chunk[step], axis, pairs)  132 us
    pallas_call x3, Pallas kernels, run_inverse(): pl.pallas_call(functools.partial(inverse_x, count, cuts, kinds, layer, fi...  40 us
    pallas_call x2, Pallas kernels, run_filter(): pl.pallas_call(functools.partial(filter_y, count, in_cuts, in_kinds, out_...  31.1 us
    pallas_call x2, Pallas kernels, run_forward(): pl.pallas_call(functools.partial(forward_x, count, cuts, kinds), grid=((l...  18.1 us
    reshape x1, local copies, waits for them, and re-layouts, arranged(): lax.optimization_barrier(table).reshape(share, RADIX, LENGTH)  11.8 us
    optimization_barrier x1, local copies, waits for them, and re-layouts, arranged(): table = lax.optimization_barrier(table).reshape(LENGTH, RADIX * share).T  11.6 us
    optimization_barrier x1, local copies, waits for them, and re-layouts, arranged(): lax.optimization_barrier(table).reshape(share, RADIX, LENGTH)  8.91 us
  transfers between devices with their start and end apart: 46, of which 14 were waited for; matrix products, arithmetic and copies ran while one was open for 8% of the time, Pallas kernels for 17%

profile of v1, /device:TPU:0, one launch (start us, length us, event | category | flops | bytes accessed | tf_op | source)
XLA Modules:
  0.0 424.7 jit_solution(1449377639423971814)
XLA Ops:
  0.6 6.5 %forward_x.2 = (f32[512,128]{1,0:T(8,128)}, f32[512,128]{1,0:T(8,128)}, f32[512,128]{1,0:T(8,128)}, f32[512,128]{1,0:T(8,128)}, f32[512,128]{1,0:T(8,128)}, /*in...) custom-call(s32[1]{0:T(128)} %bitcast.me_ref, f32[1,512,4096]{2,1,0:T(8,128)} %noise_ref.3, ...), custom_call_target="tpu_custom_call" | custom-call | flops 5175000064 | bytes 4194304 | tf_op jit(solution)/shard_map/forward_x/pallas_call | solution.py:434
  7.6 2.6 collective-permute-start.1
  10.4 2.7 collective-permute-start.3
  13.1 3.5 collective-permute-start.5
  16.6 11.6 %forward_x.3 = (f32[256,384]{1,0:T(8,128)}, f32[256,384]{1,0:T(8,128)}, f32[256,384]{1,0:T(8,128)}, f32[256,384]{1,0:T(8,128)}, f32[256,384]{1,0:T(8,128)}, /*in...) custom-call(s32[1]{0:T(128)} %bitcast.me_ref, ...), custom_call_target="tpu_custom_call" | custom-call | flops 15525000192 | bytes 12582912 | tf_op jit(solution)/shard_map/forward_x/pallas_call | solution.py:434
  28.5 5.0 %collective-permute-done.2.refs_3_ = f32[512,128]{1,0:T(8,128)S(1)} collective-permute-done((f32[512,128]{1,0:T(8,128)}, f32[512,128]{1,0:T(8,128)S(1)}, u32[]{:S(2)}, u32[]{:S(2)}) %collective-permute-start.2) | collective-permute-done | bytes 262176 | tf_op jit(solution)/shard_map/ppermute | solution.py:374
  34.1 10.2 %collective-permute-start.22 = (f32[256,384]{1,0:T(8,128)}, f32[256,384]{1,0:T(8,128)S(1)}, u32[]{:S(2)}, u32[]{:S(2)}) collective-permute-start(f32[256,384]{1,0:T(8,128)} %get-tuple-element.123), channel_id=1, source_target_pairs={{0,2},{1,3},{2,0},{3,1},{4,6},{5,7},{6,4},{7,5},{8,10},{9,11},{10,... | collective-permute-start | bytes 1179656 | tf_op jit(solution)/shard_map/ppermute | solution.py:374
  44.2 2.2 collective-permute-start.6
  46.4 17.9 %collective-permute-done.6.refs_7_ = f32[512,128]{1,0:T(8,128)S(1)} collective-permute-done((f32[512,128]{1,0:T(8,128)S(1)}, f32[512,128]{1,0:T(8,128)S(1)}, u32[]{:S(2)}, u32[]{:S(2)}) %collective-permute-start.6) | collective-permute-done | bytes 262176 | tf_op jit(solution)/shard_map/ppermute | solution.py:374
  64.4 1.7 collective-permute-start.24
  66.0 0.8 collective-permute-start.25
  66.9 1.8 collective-permute-start.26
  68.7 2.0 collective-permute-start.27
  70.6 11.6 %copy.15 = f32[32,128,512]{2,1,0:T(8,128)} copy(f32[32,128,512]{2,0,1:T(8,128)} %bitcast.32) | data formatting | bytes 16777216 | tf_op jit(solution)/shard_map/optimization_barrier | solution.py:579
  82.3 8.9 %copy.16 = f32[512,4096]{1,0:T(8,128)} copy(f32[512,4096]{0,1:T(8,128)} %bitcast.31) | data formatting | bytes 16777216 | tf_op jit(solution)/shard_map/optimization_barrier | solution.py:580
  91.3 11.8 %copy.19 = f32[16,32,4096]{2,0,1:T(8,128)} copy(f32[16,32,4096]{2,1,0:T(8,128)} %bitcast.30) | data formatting | bytes 16777216 | tf_op jit(solution)/shard_map/reshape | solution.py:580
  103.1 8.3 %collective-permute-done.24.refs_12_ = f32[256,384]{1,0:T(8,128)} collective-permute-done((f32[256,384]{1,0:T(8,128)}, f32[256,384]{1,0:T(8,128)}, u32[]{:S(2)}, u32[]{:S(2)}) %collective-permute-start.24) | collective-permute-done | bytes 393248 | tf_op jit(solution)/shard_map/ppermute | solution.py:374
  111.4 23.8 %collective-permute-done.25.refs_13_ = f32[256,384]{1,0:T(8,128)} collective-permute-done((f32[256,384]{1,0:T(8,128)}, f32[256,384]{1,0:T(8,128)}, u32[]{:S(2)}, u32[]{:S(2)}) %collective-permute-start.25) | collective-permute-done | bytes 393248 | tf_op jit(solution)/shard_map/ppermute | solution.py:374
  135.3 4.4 %collective-permute-start.13 = (f32[256,384]{1,0:T(8,128)S(1)}, f32[256,384]{1,0:T(8,128)S(1)}, u32[]{:S(2)}, u32[]{:S(2)}) collective-permute-start(f32[256,384]{1,0:T(8,128)S(1)} %copy-done.29), channel_id=1, source_target_pairs={{0,7},{1,6},{2,5},{3,4},{4,3},{5,2},{6,1},{7,0},{8,15},{9,14},{10,... | collective-permute-start | bytes 1179656 | tf_op jit(solution)/shard_map/ppermute | solution.py:374
  139.7 15.6 %filter_y.3 = (f32[256,384]{1,0:T(8,128)}, f32[256,384]{1,0:T(8,128)}, f32[256,384]{1,0:T(8,128)}, f32[256,384]{1,0:T(8,128)}, f32[256,384]{1,0:T(8,128)}, /*ind...) custom-call(s32[1]{0:T(128)} %bitcast.me_ref, ...), custom_call_target="tpu_custom_call" | custom-call | flops 18400000000 | bytes 8388608 | tf_op jit(solution)/shard_map/filter_y/pallas_call | solution.py:477
  155.4 23.2 %collective-permute-done.10.refs_12_ = f32[256,384]{1,0:T(8,128)S(1)} collective-permute-done((f32[256,384]{1,0:T(8,128)S(1)}, f32[256,384]{1,0:T(8,128)S(1)}, u32[]{:S(2)}, u32[]{:S(2)}) %collective-permute-start.10) | collective-permute-done | bytes 393248 | tf_op jit(solution)/shard_map/ppermute | solution.py:374
  178.7 7.9 %collective-permute-start.36 = (f32[256,384]{1,0:T(8,128)}, f32[256,384]{1,0:T(8,128)S(1)}, u32[]{:S(2)}, u32[]{:S(2)}) collective-permute-start(f32[256,384]{1,0:T(8,128)} %get-tuple-element.139), channel_id=1, source_target_pairs={{0,2},{1,3},{2,0},{3,1},{4,6},{5,7},{6,4},{7,5},{8,10},{9,11},{10,... | collective-permute-start | bytes 1179656 | tf_op jit(solution)/shard_map/ppermute | solution.py:374
  186.7 9.3 %collective-permute-start.38 = (f32[256,384]{1,0:T(8,128)}, f32[256,384]{1,0:T(8,128)S(1)}, u32[]{:S(2)}, u32[]{:S(2)}) collective-permute-start(f32[256,384]{1,0:T(8,128)} %get-tuple-element.141), channel_id=1, source_target_pairs={{0,4},{1,5},{2,6},{3,7},{4,0},{5,1},{6,2},{7,3},{8,12},{9,13},{10,... | collective-permute-start | bytes 1179656 | tf_op jit(solution)/shard_map/ppermute | solution.py:374
  196.8 15.5 %filter_y.2 = (f32[256,512]{1,0:T(8,128)}, f32[256,512]{1,0:T(8,128)}, f32[256,512]{1,0:T(8,128)}, f32[256,512]{1,0:T(8,128)}, f32[256,512]{1,0:T(8,128)}, /*ind...) custom-call(s32[1]{0:T(128)} %bitcast.me_ref, f32[512,128]{1,0:T(8,128)} %get-tuple-element.80.refs_0_, ...), custom_call_target="tpu_custom_call" | custom-call | flops 18400000000 | bytes 8388608 | tf_op jit(solution)/shard_map/filter_y/pallas_call | solution.py:477
  212.4 8.6 %collective-permute-start.15 = (f32[256,512]{1,0:T(8,128)}, f32[256,512]{1,0:T(8,128)S(1)}, u32[]{:S(2)}, u32[]{:S(2)}) collective-permute-start(f32[256,512]{1,0:T(8,128)} %get-tuple-element.115), channel_id=1, source_target_pairs={{0,2},{1,3},{2,0},{3,1},{4,6},{5,7},{6,4},{7,5},{8,10},{9,11},{10,... | collective-permute-start | bytes 1572872 | tf_op jit(solution)/shard_map/ppermute | solution.py:374
  221.1 2.1 collective-permute-start.40
  223.2 1.1 collective-permute-start.41
  224.3 17.6 %collective-permute-done.39.refs_13_ = f32[256,384]{1,0:T(8,128)S(1)} collective-permute-done((f32[256,384]{1,0:T(8,128)S(1)}, f32[256,384]{1,0:T(8,128)S(1)}, u32[]{:S(2)}, u32[]{:S(2)}) %collective-permute-start.39) | collective-permute-done | bytes 393248 | tf_op jit(solution)/shard_map/ppermute | solution.py:374
  242.0 1.9 collective-permute-start.16
  243.8 8.5 %collective-permute-done.40.refs_14_ = f32[256,384]{1,0:T(8,128)S(1)} collective-permute-done((f32[256,384]{1,0:T(8,128)S(1)}, f32[256,384]{1,0:T(8,128)S(1)}, u32[]{:S(2)}, u32[]{:S(2)}) %collective-permute-start.40) | collective-permute-done | bytes 393248 | tf_op jit(solution)/shard_map/ppermute | solution.py:374
  252.3 15.2 %collective-permute-start.17 = (f32[256,512]{1,0:T(8,128)}, f32[256,512]{1,0:T(8,128)S(1)}, u32[]{:S(2)}, u32[]{:S(2)}) collective-permute-start(f32[256,512]{1,0:T(8,128)} %get-tuple-element.117), channel_id=1, source_target_pairs={{0,4},{1,5},{2,6},{3,7},{4,0},{5,1},{6,2},{7,3},{8,12},{9,13},{10,... | collective-permute-start | bytes 1572872 | tf_op jit(solution)/shard_map/ppermute | solution.py:374
  267.5 19.4 %collective-permute-start.18 = (f32[256,512]{1,0:T(8,128)}, f32[256,512]{1,0:T(8,128)S(1)}, u32[]{:S(2)}, u32[]{:S(2)}) collective-permute-start(f32[256,512]{1,0:T(8,128)} %get-tuple-element.118), channel_id=1, source_target_pairs={{0,5},{1,4},{2,7},{3,6},{4,1},{5,0},{6,3},{7,2},{8,13},{9,12},{10,... | collective-permute-start | bytes 1572872 | tf_op jit(solution)/shard_map/ppermute | solution.py:374
  286.9 2.6 collective-permute-start.19
  289.5 1.1 collective-permute-start.20
  291.0 40.7 %collective-permute-done.17.refs_4_ = f32[256,512]{1,0:T(8,128)S(1)} collective-permute-done((f32[256,512]{1,0:T(8,128)}, f32[256,512]{1,0:T(8,128)S(1)}, u32[]{:S(2)}, u32[]{:S(2)}) %collective-permute-start.17) | collective-permute-done | bytes 524320 | tf_op jit(solution)/shard_map/ppermute | solution.py:374
  331.7 11.3 %collective-permute-done.18.refs_5_ = f32[256,512]{1,0:T(8,128)S(1)} collective-permute-done((f32[256,512]{1,0:T(8,128)}, f32[256,512]{1,0:T(8,128)S(1)}, u32[]{:S(2)}, u32[]{:S(2)}) %collective-permute-start.18) | collective-permute-done | bytes 524320 | tf_op jit(solution)/shard_map/ppermute | solution.py:374
  343.1 11.6 %collective-permute-start.31 = (f32[256,128]{1,0:T(8,128)}, f32[256,128]{1,0:T(8,128)S(1)}, u32[]{:S(2)}, u32[]{:S(2)}) collective-permute-start(f32[256,128]{1,0:T(8,128)} %get-tuple-element.133), channel_id=1, source_target_pairs={{0,4},{1,5},{2,6},{3,7},{4,0},{5,1},{6,2},{7,3},{8,12},{9,13},{10,... | collective-permute-start | bytes 393224 | tf_op jit(solution)/shard_map/ppermute | solution.py:374
  354.6 13.9 %collective-permute-start.32 = (f32[256,128]{1,0:T(8,128)}, f32[256,128]{1,0:T(8,128)S(1)}, u32[]{:S(2)}, u32[]{:S(2)}) collective-permute-start(f32[256,128]{1,0:T(8,128)} %get-tuple-element.134), channel_id=1, source_target_pairs={{0,5},{1,4},{2,7},{3,6},{4,1},{5,0},{6,3},{7,2},{8,13},{9,12},{10,... | collective-permute-start | bytes 393224 | tf_op jit(solution)/shard_map/ppermute | solution.py:374
  368.6 17.7 %inverse_x.3 = (f32[1,512,4096]{2,1,0:T(8,128)}, f32[1,512,4096]{2,1,0:T(8,128)}, f32[2,32,512]{2,1,0:T(8,128)}, f32[8,4096]{1,0:T(8,128)}, f32[8,4096]{1,0:T(8,128)}) custom-call(s32[1]{0:T(128)} %bitcast.me_ref, s32[2]{0:T(128)} %offsets_ref.5, f32[256,512]{1,0:T(8,128)} %get-tuple-element.113.refs_0_, f32[256,512]{1,0:T(8,128)} %copy-done.19, ...), custom_call_target="tpu_custom_call" | custom-call | flops 20700000256 | bytes 8388608 | tf_op jit(solution)/shard_map/inverse_x/pallas_call | solution.py:536
  386.3 2.6 collective-permute-start.33
  388.8 1.1 collective-permute-start.34
  390.0 2.5 collective-permute-start.42
  392.5 10.8 %inverse_x.4 = (f32[1,512,4096]{2,1,0:T(8,128)}, f32[1,512,4096]{2,1,0:T(8,128)}, f32[2,16,512]{2,1,0:T(8,128)}, f32[8,4096]{1,0:T(8,128)}, f32[8,4096]{1,0:T(8,128)}) custom-call(s32[1]{0:T(128)} %bitcast.me_ref, s32[2]{0:T(128)} %offsets_ref.5, f32[256,512]{1,0:T(8,128)} %get-tuple-element.113.refs_0_, ...), custom_call_target="tpu_custom_call", output_to_operand_aliasing={{0}: (20, {}), {1}: (21, {})} | custom-call | flops 10350000128 | bytes 4194304 | tf_op jit(solution)/shard_map/inverse_x/pallas_call | solution.py:536
  404.1 11.6 %inverse_x.5 = (f32[1,512,4096]{2,1,0:T(8,128)}, f32[1,512,4096]{2,1,0:T(8,128)}, f32[2,32,512]{2,1,0:T(8,128)}, f32[8,4096]{1,0:T(8,128)}, f32[8,4096]{1,0:T(8,128)}) custom-call(s32[1]{0:T(128)} %bitcast.me_ref, s32[2]{0:T(128)} %offsets_ref.5, f32[256,512]{1,0:T(8,128)} %get-tuple-element.113.refs_0_, ...), custom_call_target="tpu_custom_call", output_to_operand_aliasing={{0}: (21, {}), {1}: (22, {})} | custom-call | flops 10350000128 | bytes 4194304 | tf_op jit(solution)/shard_map/inverse_x/pallas_call | solution.py:536
  415.7 0.9 slice.13
  416.7 2.5 collective-permute-start.45
  420.3 1.9 collective-permute-done.45
  422.1 1.4 collective-permute-done.44
  (161 shorter events, 6.2 us)
Async XLA Ops:
  7.2 5.9 %collective-permute-start = (f32[512,128]{1,0:T(8,128)}, f32[512,128]{1,0:T(8,128)S(1)}, u32[]{:S(2)}, u32[]{:S(2)}) collective-permute-start(f32[512,128]{1,0:T(8,128)} %get-tuple-element.81), channel_id=1, source_target_pairs={{0,1},{1,0},{2,3},{3,2},{4,5},{5,4},{6,7},{7,6},{8,9},{9,8},{10,11... | collective-permute-start | bytes 786440 | tf_op jit(solution)/shard_map/ppermute | solution.py:374
  7.6 20.7 %collective-permute-start.1 = (f32[512,128]{1,0:T(8,128)}, f32[512,128]{1,0:T(8,128)S(1)}, u32[]{:S(2)}, u32[]{:S(2)}) collective-permute-start(f32[512,128]{1,0:T(8,128)} %get-tuple-element.82), channel_id=1, source_target_pairs={{0,2},{1,3},{2,0},{3,1},{4,6},{5,7},{6,4},{7,5},{8,10},{9,11},{10,... | collective-permute-start | bytes 786440 | tf_op jit(solution)/shard_map/ppermute | solution.py:374
  10.2 23.4 %collective-permute-start.2 = (f32[512,128]{1,0:T(8,128)}, f32[512,128]{1,0:T(8,128)S(1)}, u32[]{:S(2)}, u32[]{:S(2)}) collective-permute-start(f32[512,128]{1,0:T(8,128)} %get-tuple-element.83), channel_id=1, source_target_pairs={{0,3},{1,2},{2,1},{3,0},{4,7},{5,6},{6,5},{7,4},{8,11},{9,10},{10,... | collective-permute-start | bytes 786440 | tf_op jit(solution)/shard_map/ppermute | solution.py:374
  10.4 23.2 %collective-permute-start.3 = (f32[512,128]{1,0:T(8,128)}, f32[512,128]{1,0:T(8,128)S(1)}, u32[]{:S(2)}, u32[]{:S(2)}) collective-permute-start(f32[512,128]{1,0:T(8,128)} %get-tuple-element.84), channel_id=1, source_target_pairs={{0,4},{1,5},{2,6},{3,7},{4,0},{5,1},{6,2},{7,3},{8,12},{9,13},{10,... | collective-permute-start | bytes 786440 | tf_op jit(solution)/shard_map/ppermute | solution.py:374
  13.1 21.0 %collective-permute-start.4 = (f32[512,128]{1,0:T(8,128)}, f32[512,128]{1,0:T(8,128)S(1)}, u32[]{:S(2)}, u32[]{:S(2)}) collective-permute-start(f32[512,128]{1,0:T(8,128)} %get-tuple-element.85), channel_id=1, source_target_pairs={{0,5},{1,4},{2,7},{3,6},{4,1},{5,0},{6,3},{7,2},{8,13},{9,12},{10,... | collective-permute-start | bytes 786440 | tf_op jit(solution)/shard_map/ppermute | solution.py:374
  13.1 31.1 %collective-permute-start.5 = (f32[512,128]{1,0:T(8,128)}, f32[512,128]{1,0:T(8,128)S(1)}, u32[]{:S(2)}, u32[]{:S(2)}) collective-permute-start(f32[512,128]{1,0:T(8,128)} %get-tuple-element.86), channel_id=1, source_target_pairs={{0,6},{1,7},{2,4},{3,5},{4,2},{5,3},{6,0},{7,1},{8,14},{9,15},{10,... | collective-permute-start | bytes 786440 | tf_op jit(solution)/shard_map/ppermute | solution.py:374
  28.3 36.0 %collective-permute-start.7 = (f32[256,384]{1,0:T(8,128)}, f32[256,384]{1,0:T(8,128)S(1)}, u32[]{:S(2)}, u32[]{:S(2)}) collective-permute-start(f32[256,384]{1,0:T(8,128)} %get-tuple-element.105), channel_id=1, source_target_pairs={{0,1},{1,0},{2,3},{3,2},{4,5},{5,4},{6,7},{7,6},{8,9},{9,8},{10,11... | collective-permute-start | bytes 1179656 | tf_op jit(solution)/shard_map/ppermute | solution.py:374
  33.6 32.5 %collective-permute-start.8 = (f32[256,384]{1,0:T(8,128)}, f32[256,384]{1,0:T(8,128)S(1)}, u32[]{:S(2)}, u32[]{:S(2)}) collective-permute-start(f32[256,384]{1,0:T(8,128)} %get-tuple-element.106), channel_id=1, source_target_pairs={{0,2},{1,3},{2,0},{3,1},{4,6},{5,7},{6,4},{7,5},{8,10},{9,11},{10,... | collective-permute-start | bytes 1179656 | tf_op jit(solution)/shard_map/ppermute | solution.py:374
  33.6 33.3 %collective-permute-start.21 = (f32[256,384]{1,0:T(8,128)}, f32[256,384]{1,0:T(8,128)S(1)}, u32[]{:S(2)}, u32[]{:S(2)}) collective-permute-start(f32[256,384]{1,0:T(8,128)} %get-tuple-element.122), channel_id=1, source_target_pairs={{0,1},{1,0},{2,3},{3,2},{4,5},{5,4},{6,7},{7,6},{8,9},{9,8},{10,11... | collective-permute-start | bytes 1179656 | tf_op jit(solution)/shard_map/ppermute | solution.py:374
  34.1 34.6 %collective-permute-start.22 = (f32[256,384]{1,0:T(8,128)}, f32[256,384]{1,0:T(8,128)S(1)}, u32[]{:S(2)}, u32[]{:S(2)}) collective-permute-start(f32[256,384]{1,0:T(8,128)} %get-tuple-element.123), channel_id=1, source_target_pairs={{0,2},{1,3},{2,0},{3,1},{4,6},{5,7},{6,4},{7,5},{8,10},{9,11},{10,... | collective-permute-start | bytes 1179656 | tf_op jit(solution)/shard_map/ppermute | solution.py:374
  44.2 20.1 %collective-permute-start.6 = (f32[512,128]{1,0:T(8,128)S(1)}, f32[512,128]{1,0:T(8,128)S(1)}, u32[]{:S(2)}, u32[]{:S(2)}) collective-permute-start(f32[512,128]{1,0:T(8,128)S(1)} %copy-done.40), channel_id=1, source_target_pairs={{0,7},{1,6},{2,5},{3,4},{4,3},{5,2},{6,1},{7,0},{8,15},{9,14},{10,... | collective-permute-start | bytes 786440 | tf_op jit(solution)/shard_map/ppermute | solution.py:374
  64.3 38.7 %collective-permute-start.23 = (f32[256,384]{1,0:T(8,128)}, f32[256,384]{1,0:T(8,128)S(1)}, u32[]{:S(2)}, u32[]{:S(2)}) collective-permute-start(f32[256,384]{1,0:T(8,128)} %get-tuple-element.124), channel_id=1, source_target_pairs={{0,3},{1,2},{2,1},{3,0},{4,7},{5,6},{6,5},{7,4},{8,11},{9,10},{10,... | collective-permute-start | bytes 1179656 | tf_op jit(solution)/shard_map/ppermute | solution.py:374
  64.4 47.1 %collective-permute-start.24 = (f32[256,384]{1,0:T(8,128)}, f32[256,384]{1,0:T(8,128)}, u32[]{:S(2)}, u32[]{:S(2)}) collective-permute-start(f32[256,384]{1,0:T(8,128)} %get-tuple-element.125), channel_id=1, source_target_pairs={{0,4},{1,5},{2,6},{3,7},{4,0},{5,1},{6,2},{7,3},{8,12},{9,13},{10,... | collective-permute-start | bytes 1179656 | tf_op jit(solution)/shard_map/ppermute | solution.py:374
  66.0 69.2 %collective-permute-start.25 = (f32[256,384]{1,0:T(8,128)}, f32[256,384]{1,0:T(8,128)}, u32[]{:S(2)}, u32[]{:S(2)}) collective-permute-start(f32[256,384]{1,0:T(8,128)} %get-tuple-element.126), channel_id=1, source_target_pairs={{0,5},{1,4},{2,7},{3,6},{4,1},{5,0},{6,3},{7,2},{8,13},{9,12},{10,... | collective-permute-start | bytes 1179656 | tf_op jit(solution)/shard_map/ppermute | solution.py:374
  66.9 68.3 %collective-permute-start.26 = (f32[256,384]{1,0:T(8,128)}, f32[256,384]{1,0:T(8,128)}, u32[]{:S(2)}, u32[]{:S(2)}) collective-permute-start(f32[256,384]{1,0:T(8,128)} %get-tuple-element.127), channel_id=1, source_target_pairs={{0,6},{1,7},{2,4},{3,5},{4,2},{5,3},{6,0},{7,1},{8,14},{9,15},{10,... | collective-permute-start | bytes 1179656 | tf_op jit(solution)/shard_map/ppermute | solution.py:374
  68.7 66.7 %collective-permute-start.27 = (f32[256,384]{1,0:T(8,128)}, f32[256,384]{1,0:T(8,128)}, u32[]{:S(2)}, u32[]{:S(2)}) collective-permute-start(f32[256,384]{1,0:T(8,128)} %get-tuple-element.128), channel_id=1, source_target_pairs={{0,7},{1,6},{2,5},{3,4},{4,3},{5,2},{6,1},{7,0},{8,15},{9,14},{10,... | collective-permute-start | bytes 1179656 | tf_op jit(solution)/shard_map/ppermute | solution.py:374
  103.1 52.3 %collective-permute-start.9 = (f32[256,384]{1,0:T(8,128)S(1)}, f32[256,384]{1,0:T(8,128)S(1)}, u32[]{:S(2)}, u32[]{:S(2)}) collective-permute-start(f32[256,384]{1,0:T(8,128)S(1)} %copy-done.36), channel_id=1, source_target_pairs={{0,3},{1,2},{2,1},{3,0},{4,7},{5,6},{6,5},{7,4},{8,11},{9,10},{10,... | collective-permute-start | bytes 1179656 | tf_op jit(solution)/shard_map/ppermute | solution.py:374
  111.4 67.2 %collective-permute-start.10 = (f32[256,384]{1,0:T(8,128)S(1)}, f32[256,384]{1,0:T(8,128)S(1)}, u32[]{:S(2)}, u32[]{:S(2)}) collective-permute-start(f32[256,384]{1,0:T(8,128)S(1)} %copy-done.34), channel_id=1, source_target_pairs={{0,4},{1,5},{2,6},{3,7},{4,0},{5,1},{6,2},{7,3},{8,12},{9,13},{10,... | collective-permute-start | bytes 1179656 | tf_op jit(solution)/shard_map/ppermute | solution.py:374
  135.2 51.3 %collective-permute-start.11 = (f32[256,384]{1,0:T(8,128)S(1)}, f32[256,384]{1,0:T(8,128)S(1)}, u32[]{:S(2)}, u32[]{:S(2)}) collective-permute-start(f32[256,384]{1,0:T(8,128)S(1)} %copy-done.32), channel_id=1, source_target_pairs={{0,5},{1,4},{2,7},{3,6},{4,1},{5,0},{6,3},{7,2},{8,13},{9,12},{10,... | collective-permute-start | bytes 1179656 | tf_op jit(solution)/shard_map/ppermute | solution.py:374
  135.2 51.5 %collective-permute-start.12 = (f32[256,384]{1,0:T(8,128)S(1)}, f32[256,384]{1,0:T(8,128)S(1)}, u32[]{:S(2)}, u32[]{:S(2)}) collective-permute-start(f32[256,384]{1,0:T(8,128)S(1)} %copy-done.30), channel_id=1, source_target_pairs={{0,6},{1,7},{2,4},{3,5},{4,2},{5,3},{6,0},{7,1},{8,14},{9,15},{10,... | collective-permute-start | bytes 1179656 | tf_op jit(solution)/shard_map/ppermute | solution.py:374
  135.3 60.7 %collective-permute-start.13 = (f32[256,384]{1,0:T(8,128)S(1)}, f32[256,384]{1,0:T(8,128)S(1)}, u32[]{:S(2)}, u32[]{:S(2)}) collective-permute-start(f32[256,384]{1,0:T(8,128)S(1)} %copy-done.29), channel_id=1, source_target_pairs={{0,7},{1,6},{2,5},{3,4},{4,3},{5,2},{6,1},{7,0},{8,15},{9,14},{10,... | collective-permute-start | bytes 1179656 | tf_op jit(solution)/shard_map/ppermute | solution.py:374
  155.4 57.0 %collective-permute-start.35 = (f32[256,384]{1,0:T(8,128)}, f32[256,384]{1,0:T(8,128)S(1)}, u32[]{:S(2)}, u32[]{:S(2)}) collective-permute-start(f32[256,384]{1,0:T(8,128)} %get-tuple-element.138), channel_id=1, source_target_pairs={{0,1},{1,0},{2,3},{3,2},{4,5},{5,4},{6,7},{7,6},{8,9},{9,8},{10,11... | collective-permute-start | bytes 1179656 | tf_op jit(solution)/shard_map/ppermute | solution.py:374
  178.7 42.3 %collective-permute-start.36 = (f32[256,384]{1,0:T(8,128)}, f32[256,384]{1,0:T(8,128)S(1)}, u32[]{:S(2)}, u32[]{:S(2)}) collective-permute-start(f32[256,384]{1,0:T(8,128)} %get-tuple-element.139), channel_id=1, source_target_pairs={{0,2},{1,3},{2,0},{3,1},{4,6},{5,7},{6,4},{7,5},{8,10},{9,11},{10,... | collective-permute-start | bytes 1179656 | tf_op jit(solution)/shard_map/ppermute | solution.py:374
  186.6 34.5 %collective-permute-start.37 = (f32[256,384]{1,0:T(8,128)}, f32[256,384]{1,0:T(8,128)S(1)}, u32[]{:S(2)}, u32[]{:S(2)}) collective-permute-start(f32[256,384]{1,0:T(8,128)} %get-tuple-element.140), channel_id=1, source_target_pairs={{0,3},{1,2},{2,1},{3,0},{4,7},{5,6},{6,5},{7,4},{8,11},{9,10},{10,... | collective-permute-start | bytes 1179656 | tf_op jit(solution)/shard_map/ppermute | solution.py:374
  186.7 36.5 %collective-permute-start.38 = (f32[256,384]{1,0:T(8,128)}, f32[256,384]{1,0:T(8,128)S(1)}, u32[]{:S(2)}, u32[]{:S(2)}) collective-permute-start(f32[256,384]{1,0:T(8,128)} %get-tuple-element.141), channel_id=1, source_target_pairs={{0,4},{1,5},{2,6},{3,7},{4,0},{5,1},{6,2},{7,3},{8,12},{9,13},{10,... | collective-permute-start | bytes 1179656 | tf_op jit(solution)/shard_map/ppermute | solution.py:374
  212.3 74.6 %collective-permute-start.14 = (f32[256,512]{1,0:T(8,128)}, f32[256,512]{1,0:T(8,128)S(1)}, u32[]{:S(2)}, u32[]{:S(2)}) collective-permute-start(f32[256,512]{1,0:T(8,128)} %get-tuple-element.114), channel_id=1, source_target_pairs={{0,1},{1,0},{2,3},{3,2},{4,5},{5,4},{6,7},{7,6},{8,9},{9,8},{10,11... | collective-permute-start | bytes 1572872 | tf_op jit(solution)/shard_map/ppermute | solution.py:374
  212.4 156.1 %copy-start.25 = (f32[256,384]{1,0:T(8,128)}, f32[256,384]{1,0:T(8,128)S(1)}, u32[]{:S(2)}) copy-start(f32[256,384]{1,0:T(8,128)S(1)} %collective-permute-done.35.refs_9_) | copy-start | bytes 1179652
  212.4 77.1 %collective-permute-start.15 = (f32[256,512]{1,0:T(8,128)}, f32[256,512]{1,0:T(8,128)S(1)}, u32[]{:S(2)}, u32[]{:S(2)}) collective-permute-start(f32[256,512]{1,0:T(8,128)} %get-tuple-element.115), channel_id=1, source_target_pairs={{0,2},{1,3},{2,0},{3,1},{4,6},{5,7},{6,4},{7,5},{8,10},{9,11},{10,... | collective-permute-start | bytes 1572872 | tf_op jit(solution)/shard_map/ppermute | solution.py:374
  221.0 21.0 %collective-permute-start.39 = (f32[256,384]{1,0:T(8,128)S(1)}, f32[256,384]{1,0:T(8,128)S(1)}, u32[]{:S(2)}, u32[]{:S(2)}) collective-permute-start(f32[256,384]{1,0:T(8,128)S(1)} %copy-done.39), channel_id=1, source_target_pairs={{0,5},{1,4},{2,7},{3,6},{4,1},{5,0},{6,3},{7,2},{8,13},{9,12},{10,... | collective-permute-start | bytes 1179656 | tf_op jit(solution)/shard_map/ppermute | solution.py:374
  221.1 31.2 %collective-permute-start.40 = (f32[256,384]{1,0:T(8,128)S(1)}, f32[256,384]{1,0:T(8,128)S(1)}, u32[]{:S(2)}, u32[]{:S(2)}) collective-permute-start(f32[256,384]{1,0:T(8,128)S(1)} %copy-done.38), channel_id=1, source_target_pairs={{0,6},{1,7},{2,4},{3,5},{4,2},{5,3},{6,0},{7,1},{8,14},{9,15},{10,... | collective-permute-start | bytes 1179656 | tf_op jit(solution)/shard_map/ppermute | solution.py:374
  223.2 44.3 %collective-permute-start.41 = (f32[256,384]{1,0:T(8,128)S(1)}, f32[256,384]{1,0:T(8,128)S(1)}, u32[]{:S(2)}, u32[]{:S(2)}) collective-permute-start(f32[256,384]{1,0:T(8,128)S(1)} %copy-done.37), channel_id=1, source_target_pairs={{0,7},{1,6},{2,5},{3,4},{4,3},{5,2},{6,1},{7,0},{8,15},{9,14},{10,... | collective-permute-start | bytes 1179656 | tf_op jit(solution)/shard_map/ppermute | solution.py:374
  242.0 48.6 %collective-permute-start.16 = (f32[256,512]{1,0:T(8,128)}, f32[256,512]{1,0:T(8,128)S(1)}, u32[]{:S(2)}, u32[]{:S(2)}) collective-permute-start(f32[256,512]{1,0:T(8,128)} %get-tuple-element.116), channel_id=1, source_target_pairs={{0,3},{1,2},{2,1},{3,0},{4,7},{5,6},{6,5},{7,4},{8,11},{9,10},{10,... | collective-permute-start | bytes 1572872 | tf_op jit(solution)/shard_map/ppermute | solution.py:374
  252.3 79.4 %collective-permute-start.17 = (f32[256,512]{1,0:T(8,128)}, f32[256,512]{1,0:T(8,128)S(1)}, u32[]{:S(2)}, u32[]{:S(2)}) collective-permute-start(f32[256,512]{1,0:T(8,128)} %get-tuple-element.117), channel_id=1, source_target_pairs={{0,4},{1,5},{2,6},{3,7},{4,0},{5,1},{6,2},{7,3},{8,12},{9,13},{10,... | collective-permute-start | bytes 1572872 | tf_op jit(solution)/shard_map/ppermute | solution.py:374
  267.5 75.5 %collective-permute-start.18 = (f32[256,512]{1,0:T(8,128)}, f32[256,512]{1,0:T(8,128)S(1)}, u32[]{:S(2)}, u32[]{:S(2)}) collective-permute-start(f32[256,512]{1,0:T(8,128)} %get-tuple-element.118), channel_id=1, source_target_pairs={{0,5},{1,4},{2,7},{3,6},{4,1},{5,0},{6,3},{7,2},{8,13},{9,12},{10,... | collective-permute-start | bytes 1572872 | tf_op jit(solution)/shard_map/ppermute | solution.py:374
  286.9 81.6 %copy-start.19 = (f32[256,512]{1,0:T(8,128)}, f32[256,512]{1,0:T(8,128)S(1)}, u32[]{:S(2)}) copy-start(f32[256,512]{1,0:T(8,128)S(1)} %collective-permute-done.14.refs_1_) | copy-start | bytes 1572868
  286.9 56.2 %collective-permute-start.19 = (f32[256,512]{1,0:T(8,128)}, f32[256,512]{1,0:T(8,128)S(1)}, u32[]{:S(2)}, u32[]{:S(2)}) collective-permute-start(f32[256,512]{1,0:T(8,128)} %get-tuple-element.119), channel_id=1, source_target_pairs={{0,6},{1,7},{2,4},{3,5},{4,2},{5,3},{6,0},{7,1},{8,14},{9,15},{10,... | collective-permute-start | bytes 1572872 | tf_op jit(solution)/shard_map/ppermute | solution.py:374
  289.5 65.1 %collective-permute-start.20 = (f32[256,512]{1,0:T(8,128)}, f32[256,512]{1,0:T(8,128)}, u32[]{:S(2)}, u32[]{:S(2)}) collective-permute-start(f32[256,512]{1,0:T(8,128)} %get-tuple-element.120), channel_id=1, source_target_pairs={{0,7},{1,6},{2,5},{3,4},{4,3},{5,2},{6,1},{7,0},{8,15},{9,14},{10,... | collective-permute-start | bytes 1572872 | tf_op jit(solution)/shard_map/ppermute | solution.py:374
  290.6 95.6 %collective-permute-start.28 = (f32[256,128]{1,0:T(8,128)}, f32[256,128]{1,0:T(8,128)S(1)}, u32[]{:S(2)}, u32[]{:S(2)}) collective-permute-start(f32[256,128]{1,0:T(8,128)} %get-tuple-element.130), channel_id=1, source_target_pairs={{0,1},{1,0},{2,3},{3,2},{4,5},{5,4},{6,7},{7,6},{8,9},{9,8},{10,11... | collective-permute-start | bytes 393224 | tf_op jit(solution)/shard_map/ppermute | solution.py:374
  331.7 57.1 %collective-permute-start.29 = (f32[256,128]{1,0:T(8,128)}, f32[256,128]{1,0:T(8,128)S(1)}, u32[]{:S(2)}, u32[]{:S(2)}) collective-permute-start(f32[256,128]{1,0:T(8,128)} %get-tuple-element.131), channel_id=1, source_target_pairs={{0,2},{1,3},{2,0},{3,1},{4,6},{5,7},{6,4},{7,5},{8,10},{9,11},{10,... | collective-permute-start | bytes 393224 | tf_op jit(solution)/shard_map/ppermute | solution.py:374
  343.0 46.9 %collective-permute-start.30 = (f32[256,128]{1,0:T(8,128)}, f32[256,128]{1,0:T(8,128)S(1)}, u32[]{:S(2)}, u32[]{:S(2)}) collective-permute-start(f32[256,128]{1,0:T(8,128)} %get-tuple-element.132), channel_id=1, source_target_pairs={{0,3},{1,2},{2,1},{3,0},{4,7},{5,6},{6,5},{7,4},{8,11},{9,10},{10,... | collective-permute-start | bytes 393224 | tf_op jit(solution)/shard_map/ppermute | solution.py:374
  343.1 60.2 %collective-permute-start.31 = (f32[256,128]{1,0:T(8,128)}, f32[256,128]{1,0:T(8,128)S(1)}, u32[]{:S(2)}, u32[]{:S(2)}) collective-permute-start(f32[256,128]{1,0:T(8,128)} %get-tuple-element.133), channel_id=1, source_target_pairs={{0,4},{1,5},{2,6},{3,7},{4,0},{5,1},{6,2},{7,3},{8,12},{9,13},{10,... | collective-permute-start | bytes 393224 | tf_op jit(solution)/shard_map/ppermute | solution.py:374
  354.6 48.6 %collective-permute-start.32 = (f32[256,128]{1,0:T(8,128)}, f32[256,128]{1,0:T(8,128)S(1)}, u32[]{:S(2)}, u32[]{:S(2)}) collective-permute-start(f32[256,128]{1,0:T(8,128)} %get-tuple-element.134), channel_id=1, source_target_pairs={{0,5},{1,4},{2,7},{3,6},{4,1},{5,0},{6,3},{7,2},{8,13},{9,12},{10,... | collective-permute-start | bytes 393224 | tf_op jit(solution)/shard_map/ppermute | solution.py:374
  386.3 17.0 %collective-permute-start.33 = (f32[256,128]{1,0:T(8,128)S(1)}, f32[256,128]{1,0:T(8,128)S(1)}, u32[]{:S(2)}, u32[]{:S(2)}) collective-permute-start(f32[256,128]{1,0:T(8,128)S(1)} %copy-done.42), channel_id=1, source_target_pairs={{0,6},{1,7},{2,4},{3,5},{4,2},{5,3},{6,0},{7,1},{8,14},{9,15},{10,... | collective-permute-start | bytes 393224 | tf_op jit(solution)/shard_map/ppermute | solution.py:374
  388.8 14.5 %collective-permute-start.34 = (f32[256,128]{1,0:T(8,128)S(1)}, f32[256,128]{1,0:T(8,128)S(1)}, u32[]{:S(2)}, u32[]{:S(2)}) collective-permute-start(f32[256,128]{1,0:T(8,128)S(1)} %copy-done.41), channel_id=1, source_target_pairs={{0,7},{1,6},{2,5},{3,4},{4,3},{5,2},{6,1},{7,0},{8,15},{9,14},{10,... | collective-permute-start | bytes 393224 | tf_op jit(solution)/shard_map/ppermute | solution.py:374
  390.0 13.4 %collective-permute-start.42 = (f32[8,4096]{1,0:T(8,128)}, f32[8,4096]{1,0:T(8,128)S(1)}, u32[]{:S(2)}, u32[]{:S(2)}) collective-permute-start(f32[8,4096]{1,0:T(8,128)} %get-tuple-element.149), channel_id=1, source_target_pairs={{0,7},{1,0},{2,1},{3,2},{4,3},{5,4},{6,5},{7,6},{8,15},{9,8},{10,9... | collective-permute-start | bytes 393224 | tf_op jit(solution)/shard_map/ppermute | solution.py:642
  416.7 5.4 %collective-permute-start.45 = (f32[2,64,128]{2,1,0:T(8,128)S(1)}, f32[2,64,128]{2,1,0:T(8,128)S(1)}, u32[]{:S(2)}, u32[]{:S(2)}) collective-permute-start(f32[2,64,128]{2,1,0:T(8,128)S(1)} %get-tuple-element.158), channel_id=1, source_target_pairs={{0,24},{8,16},{16,8},{24,0},{1,25},{9,17},{17,9},{25,1},{2,26},{10... | collective-permute-start | bytes 196616 | tf_op jit(solution)/shard_map/ppermute | solution.py:590
  419.2 4.3 %collective-permute-start.44 = (f32[2,64,128]{2,1,0:T(8,128)S(1)}, f32[2,64,128]{2,1,0:T(8,128)S(1)}, u32[]{:S(2)}, u32[]{:S(2)}) collective-permute-start(f32[2,64,128]{2,1,0:T(8,128)S(1)} %get-tuple-element.159), channel_id=1, source_target_pairs={{0,16},{8,24},{16,0},{24,8},{1,17},{9,25},{17,1},{25,9},{2,18},{10... | collective-permute-start | bytes 196616 | tf_op jit(solution)/shard_map/ppermute | solution.py:590
  419.7 4.3 %collective-permute-start.43 = (f32[2,64,128]{2,1,0:T(8,128)S(1)}, f32[2,64,128]{2,1,0:T(8,128)S(1)}, u32[]{:S(2)}, u32[]{:S(2)}) collective-permute-start(f32[2,64,128]{2,1,0:T(8,128)S(1)} %get-tuple-element.157), channel_id=1, source_target_pairs={{0,8},{8,0},{16,24},{24,16},{1,9},{9,1},{17,25},{25,17},{2,10},{10... | collective-permute-start | bytes 196616 | tf_op jit(solution)/shard_map/ppermute | solution.py:590
  (49 other events, 1257.4 us)

commit v2 on v1

--- a/solution.py
+++ b/solution.py
@@ -16,6 +16,8 @@
 LENGTH = RADIX * LANES
 PAIR = 2 * LANES
 BLOCK = 8
+BATCH = 4
+PARTS = 4
 VMEM_BYTES = 56 * 1024 * 1024
 
 CLASSES = [(0, RADIX // 2)] + [(k, RADIX - k) for k in range(1, GROUPS)]
@@ -146,6 +148,12 @@
     return slice(index * LANES, (index + 1) * LANES)
 
 
+def step_order(count):
+    half = count // 2
+    pairs = [(near, half + near) for near in range(half)]
+    return [0] + [step for pair in pairs[1:] for step in pair] + [half]
+
+
 def taken(refs, kinds, count):
     chunks = []
     for stacked in kinds:
@@ -158,7 +166,7 @@
 def view(chunk, stacked, me, step):
     if stacked:
         return step, chunk[0].at[step]
-    return me ^ step, chunk[step]
+    return me ^ step_order(len(chunk))[step], chunk[step]
 
 
 def forward_x(count, cuts, kinds, me_ref, noise_ref, table_ref, *refs):
@@ -242,19 +250,17 @@
 
 
 def inverse_x(
-    count, cuts, kinds, layer, start, has_before, has_after, aliased, me_ref, offsets_ref, *refs
+    count, cuts, kinds, lanes, layer, start, has_before, has_after, aliased, me_ref, offsets_ref, *refs
 ):
     ins, refs = taken(refs, kinds, count)
-    table_ref, refs = refs[0], refs[1:]
-    before_ref = after_ref = None
-    if has_before:
-        before_ref, refs = refs[0], refs[1:]
-    if has_after:
-        after_ref, refs = refs[0], refs[1:]
+    table_hbm, refs = refs[0], refs[1:]
+    edges = has_before + has_after
+    edge_hbm, refs = refs[:edges], refs[edges:]
     if aliased:
         refs = refs[2:]
     face_x_hbm, face_y_hbm, sums_ref, first_ref, last_ref, *scratch = refs
-    piece_ref, group_ref, upper_ref, lower_ref, face_x, face_y, column_ref, sems = scratch
+    piece_ref, table_ref, edge_ref, group_ref, upper_ref, lower_ref = scratch[:6]
+    face_x, face_y, column_ref, in_sems, edge_sems, out_sems = scratch[6:]
     rows = face_x.shape[0]
     tiles = rows // BLOCK
     share = LANES // count
@@ -263,11 +269,39 @@
     made = tiles - 1 + lead + (1 if has_after else 0)
     width = RADIX * LANES
 
-    for chunk, stacked, (first, last) in zip(ins, kinds, cuts):
-        span = slice(2 * share * first, 2 * share * last)
+    def arrivals(batch):
+        group = BATCH * batch
+        copies = [
+            pltpu.make_async_copy(
+                table_hbm.at[part, pl.ds(group, BATCH)],
+                table_ref.at[part, pl.ds(group, BATCH)],
+                in_sems.at[batch, part],
+            )
+            for part in range(2)
+        ]
+        cut = max(number for number in range(len(cuts)) if cuts[number][0] <= group)
+        depth = 2 * share * BATCH
         for step in range(count):
-            place, piece = view(chunk, stacked, me, step)
-            piece_ref[place, span, :] = piece[...]
+            place, piece = view(ins[cut], kinds[cut], me, step)
+            copies.append(
+                pltpu.make_async_copy(
+                    piece.at[
+                        pl.ds(2 * share * (group - cuts[cut][0]), depth), pl.ds(lanes[cut], rows)
+                    ],
+                    piece_ref.at[place, pl.ds(2 * share * group, depth), :],
+                    in_sems.at[batch, 2 + step],
+                )
+            )
+        return copies
+
+    batches = [arrivals(batch) for batch in range(GROUPS // BATCH)]
+    edge_copies = [
+        pltpu.make_async_copy(edge_hbm[edge], edge_ref.at[edge], edge_sems.at[edge])
+        for edge in range(edges)
+    ]
+    for copies in batches + [edge_copies]:
+        for copy in copies:
+            copy.start()
 
     def group_step(group, carry):
         parts = []
@@ -278,7 +312,10 @@
         group_ref[group] = times_table(stacked.T, table_ref, group)
         return carry
 
-    lax.fori_loop(0, GROUPS, group_step, 0, unroll=4)
+    for batch, copies in enumerate(batches):
+        for copy in copies:
+            copy.wait()
+        lax.fori_loop(BATCH * batch, BATCH * (batch + 1), group_step, 0, unroll=BATCH)
 
     def raised(field, at, a):
         upper_ref[at, lanes_of(a)] = jnp.exp(field)
@@ -296,12 +333,14 @@
     field_strip(0, 0, first_ref)
     lax.fori_loop(1, tiles - 1, field_strip, 0, unroll=2)
     field_strip(tiles - 1, 0, last_ref)
+    for copy in edge_copies:
+        copy.wait()
     for a in range(RADIX):
         if has_before:
-            raised(before_ref[:, lanes_of(a)], slice(0, BLOCK), a)
+            raised(edge_ref[0, :, lanes_of(a)], slice(0, BLOCK), a)
         if has_after:
             end = (lead + tiles) * BLOCK
-            raised(after_ref[:, lanes_of(a)], slice(end, end + BLOCK), a)
+            raised(edge_ref[edges - 1, :, lanes_of(a)], slice(end, end + BLOCK), a)
 
     row_index = lax.broadcasted_iota(jnp.int32, (BLOCK, LANES), 0)
     lane_index = lax.broadcasted_iota(jnp.int32, (BLOCK, LANES), 1)
@@ -317,12 +356,6 @@
             beside = jnp.where(last_lane, moved[(a + 1) % RADIX], moved[a])
             face_x[at, lanes_of(a)] = 2.0 / (here[a] + beside)
         return carry
-
-    lax.fori_loop(0, tiles, x_strip, 0, unroll=2)
-    copy_x = pltpu.make_async_copy(
-        face_x, face_x_hbm.at[layer, pl.ds(start, rows), :], sems.at[0]
-    )
-    copy_x.start()
 
     def add_row(kind, index, a, value):
         at = strip_at(index // BLOCK)
@@ -343,11 +376,22 @@
             add_row(0, index, a, jnp.where(own_rows, here, below))
         return carry
 
-    lax.fori_loop(0, made, y_strip, 0, unroll=2)
-    copy_y = pltpu.make_async_copy(
-        face_y, face_y_hbm.at[layer, pl.ds(start - BLOCK * lead, made * BLOCK), :], sems.at[1]
-    )
-    copy_y.start()
+    leaving = []
+    faces = [(x_strip, tiles, start, face_x, face_x_hbm)]
+    faces.append((y_strip, made, start - BLOCK * lead, face_y, face_y_hbm))
+    for part in range(PARTS):
+        for number, (strip, total, origin, face, face_hbm) in enumerate(faces):
+            begin = part * (tiles // PARTS)
+            end = total if part == PARTS - 1 else begin + tiles // PARTS
+            lax.fori_loop(begin, end, strip, 0, unroll=2)
+            size = BLOCK * (end - begin)
+            copy = pltpu.make_async_copy(
+                face.at[pl.ds(BLOCK * begin, size), :],
+                face_hbm.at[layer, pl.ds(origin + BLOCK * begin, size), :],
+                out_sems.at[number, part],
+            )
+            copy.start()
+            leaving.append(copy)
 
     column_ref[:, :, width:] = column_ref[:, :, :LANES]
     reach = BLOCK * LANES + LANES
@@ -360,18 +404,18 @@
             at = BLOCK * LANES * part
             high, low = halves(column_ref[kind, :, at : at + reach])
             sums_ref[kind, :, lanes_of(part)] = dot(high, chosen) + dot(low, chosen)
-    copy_x.wait()
-    copy_y.wait()
+    for copy in leaving:
+        copy.wait()
 
 
 def exchange(chunk, axis):
     if not isinstance(chunk, list):
         return lax.all_to_all(chunk, axis, 0, 0, tiled=True)
     count = len(chunk)
-    arrived = [chunk[0]] + [None] * (count - 1)
-    for step in reversed(range(1, count)):
+    arrived = [chunk[0]]
+    for piece, step in zip(chunk[1:], step_order(count)[1:]):
         pairs = [(device, device ^ step) for device in range(count)]
-        arrived[step] = lax.ppermute(chunk[step], axis, pairs)
+        arrived.append(lax.ppermute(piece, axis, pairs))
     return arrived
 
 
@@ -515,21 +559,13 @@
     held = tiles + (before is not None) + (after is not None)
     kinds = kinds_of(chunks)
     extra = [value for value in (before, after) if value is not None]
-    in_specs = [scalars(), scalars()]
-    in_specs += block_specs(
-        kinds,
-        count,
-        [(flat([chunk])[0].shape[-2], rows) for chunk in chunks],
-        lambda n: lambda i: (0, lane_starts[n] // rows),
-    )
-    in_specs += [
-        pl.BlockSpec(table.shape, lambda i: (0, 0, 0, 0)),
-        *[pl.BlockSpec(value.shape, lambda i: (0, 0)) for value in extra],
-    ]
+    outside = pl.BlockSpec(memory_space=pl.ANY)
+    inside = pl.BlockSpec(memory_space=pltpu.VMEM)
+    in_specs = [scalars(), scalars()] + [outside] * (len(flat(chunks)) + 1 + len(extra))
     aliases = {}
     if faces is not None:
         aliases = {len(in_specs): 0, len(in_specs) + 1: 1}
-        in_specs += [pl.BlockSpec(memory_space=pl.ANY)] * 2
+        in_specs += [outside] * 2
     face = jax.ShapeDtypeStruct(shape, jnp.float32)
     tile = jax.ShapeDtypeStruct((BLOCK, LENGTH), jnp.float32)
     sums_shape = (2, padded, LENGTH // BLOCK)
@@ -539,31 +575,29 @@
             count,
             cuts,
             kinds,
+            lane_starts,
             layer,
             first,
             before is not None,
             after is not None,
             faces is not None,
         ),
-        grid=(1,),
         in_specs=in_specs,
-        out_specs=[
-            pl.BlockSpec(memory_space=pl.ANY),
-            pl.BlockSpec(memory_space=pl.ANY),
-            pl.BlockSpec(sums_shape, lambda i: (0, 0, 0)),
-            pl.BlockSpec(tile.shape, lambda i: (0, 0)),
-            pl.BlockSpec(tile.shape, lambda i: (0, 0)),
-        ],
+        out_specs=[outside, outside, inside, inside, inside],
         out_shape=[face, face, jax.ShapeDtypeStruct(sums_shape, jnp.float32), tile, tile],
         scratch_shapes=[
             pltpu.VMEM((count, LENGTH // count, rows), jnp.float32),
+            pltpu.VMEM(table.shape, table.dtype),
+            pltpu.VMEM((max(len(extra), 1), BLOCK, LENGTH), jnp.float32),
             pltpu.VMEM((GROUPS, rows, PAIR), jnp.float32),
             pltpu.VMEM((held * BLOCK, LENGTH), jnp.float32),
             pltpu.VMEM((held * BLOCK, LENGTH), jnp.float32),
             pltpu.VMEM((rows, LENGTH), jnp.float32),
             pltpu.VMEM((made * BLOCK, LENGTH), jnp.float32),
             pltpu.VMEM((2, padded, LENGTH + LANES), jnp.float32),
+            pltpu.SemaphoreType.DMA((GROUPS // BATCH, 2 + count)),
             pltpu.SemaphoreType.DMA((2,)),
+            pltpu.SemaphoreType.DMA((2, PARTS)),
         ],
         input_output_aliases=aliases,
         compiler_params=params(),
@@ -598,9 +632,9 @@
     me = lax.axis_index("gy").reshape(1)
     analysis, ahead, back = [jnp.asarray(table) for table in tables()]
     arrive_spans = [(0, LANES), (LANES, rows)]
-    leave_spans = [(0, rows - LANES), (rows - LANES, rows)]
-    done_spans = [(at, min(at + 2 * LANES, rows - LANES)) for at in range(0, rows - LANES, 2 * LANES)]
-    done_spans.append((rows - LANES, rows))
+    half = rows // 2
+    leave_spans = [(0, half), (half, rows)]
+    done_spans = leave_spans
     cuts = [(0, GROUPS // 2), (GROUPS // 2, GROUPS)]
     every = [(0, GROUPS)]
     gain = None

time: 425 us -> 405 us (0.953)
  starting transfers between devices: 138 us -> 105 us
  waiting for transfers between devices: 161 us -> 182 us
  Pallas kernels: 89.2 us -> 80 us
    ppermute x42, starting transfers between devices: 132 us -> 99.5 us  [exchange(): arrived.append(lax.ppermute(piece, axis, pairs))]
    ppermute x42, waiting for transfers between devices: 157 us -> 177 us  [exchange(): arrived.append(lax.ppermute(piece, axis, pairs))]
    pallas_call x3 -> x2, Pallas kernels: 40 us -> 30.8 us  [run_inverse(): pl.pallas_call(functools.partial(inverse_x, count, cuts, kinds, lane_star...]
  transfers between devices with their start and end apart: 46 -> 46, of which waited for: 14 -> 15; matrix products, arithmetic and copies ran while one was open for 8% -> 8% of each run, Pallas kernels for 17% -> 14%
where the time goes in v2:
time: 405 us; the launch traced here: 404 us
  waiting for transfers between devices  182 us (45%)
  starting transfers between devices  105 us (26%)
  Pallas kernels  80 us (20%)
  local copies, waits for them, and re-layouts  35.4 us (9%)
    ppermute x42, waiting for transfers between devices, exchange(): arrived.append(lax.ppermute(piece, axis, pairs))  177 us
    ppermute x42, starting transfers between devices, exchange(): arrived.append(lax.ppermute(piece, axis, pairs))  99.5 us
    pallas_call x2, Pallas kernels, run_filter(): pl.pallas_call(functools.partial(filter_y, count, in_cuts, in_kinds, out_...  31.2 us
    pallas_call x2, Pallas kernels, run_inverse(): pl.pallas_call(functools.partial(inverse_x, count, cuts, kinds, lane_star...  30.8 us
    pallas_call x2, Pallas kernels, run_forward(): pl.pallas_call(functools.partial(forward_x, count, cuts, kinds), grid=((l...  18.1 us
    reshape x1, local copies, waits for them, and re-layouts, arranged(): lax.optimization_barrier(table).reshape(share, RADIX, LENGTH)  11.8 us
    optimization_barrier x1, local copies, waits for them, and re-layouts, arranged(): table = lax.optimization_barrier(table).reshape(LENGTH, RADIX * share).T  11.6 us
    optimization_barrier x1, local copies, waits for them, and re-layouts, arranged(): lax.optimization_barrier(table).reshape(share, RADIX, LENGTH)  8.91 us
  transfers between devices with their start and end apart: 46, of which 15 were waited for; matrix products, arithmetic and copies ran while one was open for 8% of the time, Pallas kernels for 14%

profile of v2, /device:TPU:0, one launch (start us, length us, event | category | flops | bytes accessed | tf_op | source)
XLA Modules:
  0.0 404.4 jit_solution(13762116267918646652)
XLA Ops:
  0.6 6.5 %forward_x.2 = (f32[512,128]{1,0:T(8,128)}, f32[512,128]{1,0:T(8,128)}, f32[512,128]{1,0:T(8,128)}, f32[512,128]{1,0:T(8,128)}, f32[512,128]{1,0:T(8,128)}, /*in...) custom-call(s32[1]{0:T(128)} %bitcast.me_ref, f32[1,512,4096]{2,1,0:T(8,128)} %noise_ref.3, ...), custom_call_target="tpu_custom_call" | custom-call | flops 5175000064 | bytes 4194304 | tf_op jit(solution)/shard_map/forward_x/pallas_call | solution.py:478
  7.6 3.7 collective-permute-start.1
  11.3 1.6 collective-permute-start.2
  12.9 3.1 collective-permute-start.5
  16.0 11.5 %forward_x.3 = (f32[256,384]{1,0:T(8,128)}, f32[256,384]{1,0:T(8,128)}, f32[256,384]{1,0:T(8,128)}, f32[256,384]{1,0:T(8,128)}, f32[256,384]{1,0:T(8,128)}, /*in...) custom-call(s32[1]{0:T(128)} %bitcast.me_ref, ...), custom_call_target="tpu_custom_call" | custom-call | flops 15525000192 | bytes 12582912 | tf_op jit(solution)/shard_map/forward_x/pallas_call | solution.py:478
  28.9 2.4 collective-permute-done.3.refs_4_
  31.3 5.1 %collective-permute-start.23 = (f32[256,384]{1,0:T(8,128)}, f32[256,384]{1,0:T(8,128)S(1)}, u32[]{:S(2)}, u32[]{:S(2)}) collective-permute-start(f32[256,384]{1,0:T(8,128)} %get-tuple-element.120), channel_id=1, source_target_pairs={{0,2},{1,3},{2,0},{3,1},{4,6},{5,7},{6,4},{7,5},{8,10},{9,11},{10,... | collective-permute-start | bytes 1179656 | tf_op jit(solution)/shard_map/ppermute | solution.py:418
  36.5 3.5 collective-permute-start.24
  40.0 1.6 collective-permute-done.5.refs_6_
  41.6 15.8 %collective-permute-start.6 = (f32[512,128]{1,0:T(8,128)S(1)}, f32[512,128]{1,0:T(8,128)S(1)}, u32[]{:S(2)}, u32[]{:S(2)}) collective-permute-start(f32[512,128]{1,0:T(8,128)S(1)} %copy-done.45), channel_id=1, source_target_pairs={{0,4},{1,5},{2,6},{3,7},{4,0},{5,1},{6,2},{7,3},{8,12},{9,13},{10,... | collective-permute-start | bytes 786440 | tf_op jit(solution)/shard_map/ppermute | solution.py:418
  57.4 34.0 %collective-permute-done.6.refs_7_ = f32[512,128]{1,0:T(8,128)S(1)} collective-permute-done((f32[512,128]{1,0:T(8,128)S(1)}, f32[512,128]{1,0:T(8,128)S(1)}, u32[]{:S(2)}, u32[]{:S(2)}) %collective-permute-start.6) | collective-permute-done | bytes 262176 | tf_op jit(solution)/shard_map/ppermute | solution.py:418
  91.7 2.9 collective-permute-start.26
  95.2 2.9 collective-permute-start.10
  98.1 11.6 %copy.13 = f32[32,128,512]{2,1,0:T(8,128)} copy(f32[32,128,512]{2,0,1:T(8,128)} %bitcast.32) | data formatting | bytes 16777216 | tf_op jit(solution)/shard_map/optimization_barrier | solution.py:613
  109.8 8.9 %copy.14 = f32[512,4096]{1,0:T(8,128)} copy(f32[512,4096]{0,1:T(8,128)} %bitcast.31) | data formatting | bytes 16777216 | tf_op jit(solution)/shard_map/optimization_barrier | solution.py:614
  118.8 11.8 %copy.17 = f32[16,32,4096]{2,0,1:T(8,128)} copy(f32[16,32,4096]{2,1,0:T(8,128)} %bitcast.30) | data formatting | bytes 16777216 | tf_op jit(solution)/shard_map/reshape | solution.py:614
  131.3 2.5 collective-permute-start.13
  133.8 22.2 %collective-permute-done.27.refs_15_ = f32[256,384]{1,0:T(8,128)} collective-permute-done((f32[256,384]{1,0:T(8,128)}, f32[256,384]{1,0:T(8,128)}, u32[]{:S(2)}, u32[]{:S(2)}) %collective-permute-start.27) | collective-permute-done | bytes 393248 | tf_op jit(solution)/shard_map/ppermute | solution.py:418
  156.0 8.9 %collective-permute-start.8 = (f32[256,384]{1,0:T(8,128)S(1)}, f32[256,384]{1,0:T(8,128)S(1)}, u32[]{:S(2)}, u32[]{:S(2)}) collective-permute-start(f32[256,384]{1,0:T(8,128)S(1)} %copy-done.26), channel_id=1, source_target_pairs={{0,5},{1,4},{2,7},{3,6},{4,1},{5,0},{6,3},{7,2},{8,13},{9,12},{10,... | collective-permute-start | bytes 1179656 | tf_op jit(solution)/shard_map/ppermute | solution.py:418
  165.0 15.6 %filter_y.3 = (f32[256,256]{1,0:T(8,128)}, f32[256,256]{1,0:T(8,128)}, f32[256,256]{1,0:T(8,128)}, f32[256,256]{1,0:T(8,128)}, f32[256,256]{1,0:T(8,128)}, /*ind...) custom-call(s32[1]{0:T(128)} %bitcast.me_ref, ...), custom_call_target="tpu_custom_call" | custom-call | flops 18400000000 | bytes 8388608 | tf_op jit(solution)/shard_map/filter_y/pallas_call | solution.py:521
  180.6 1.6 collective-permute-start.35
  182.2 7.3 %collective-permute-done.13.refs_15_ = f32[256,384]{1,0:T(8,128)S(1)} collective-permute-done((f32[256,384]{1,0:T(8,128)S(1)}, f32[256,384]{1,0:T(8,128)S(1)}, u32[]{:S(2)}, u32[]{:S(2)}) %collective-permute-start.13) | collective-permute-done | bytes 393248 | tf_op jit(solution)/shard_map/ppermute | solution.py:418
  189.6 2.0 collective-permute-start.37
  191.6 11.6 %collective-permute-done.8.refs_10_ = f32[256,384]{1,0:T(8,128)S(1)} collective-permute-done((f32[256,384]{1,0:T(8,128)S(1)}, f32[256,384]{1,0:T(8,128)S(1)}, u32[]{:S(2)}, u32[]{:S(2)}) %collective-permute-start.8) | collective-permute-done | bytes 393248 | tf_op jit(solution)/shard_map/ppermute | solution.py:418
  203.3 2.2 collective-permute-start.38
  205.6 1.5 collective-permute-start.40
  207.1 15.6 %filter_y.2 = (f32[256,512]{1,0:T(8,128)}, f32[256,512]{1,0:T(8,128)}, f32[256,512]{1,0:T(8,128)}, f32[256,512]{1,0:T(8,128)}, f32[256,512]{1,0:T(8,128)}, /*ind...) custom-call(s32[1]{0:T(128)} %bitcast.me_ref, f32[512,128]{1,0:T(8,128)} %get-tuple-element.76.refs_0_, ...), custom_call_target="tpu_custom_call" | custom-call | flops 18400000000 | bytes 8388608 | tf_op jit(solution)/shard_map/filter_y/pallas_call | solution.py:521
  223.1 2.1 collective-permute-start.15
  225.2 3.0 collective-permute-start.41
  228.3 21.8 %collective-permute-start.29 = (f32[256,256]{1,0:T(8,128)S(1)}, f32[256,256]{1,0:T(8,128)S(1)}, u32[]{:S(2)}, u32[]{:S(2)}) collective-permute-start(f32[256,256]{1,0:T(8,128)S(1)} %copy-done.40), channel_id=1, source_target_pairs={{0,5},{1,4},{2,7},{3,6},{4,1},{5,0},{6,3},{7,2},{8,13},{9,12},{10,... | collective-permute-start | bytes 786440 | tf_op jit(solution)/shard_map/ppermute | solution.py:418
  250.1 21.0 %collective-permute-done.41.refs_15_ = f32[256,256]{1,0:T(8,128)S(1)} collective-permute-done((f32[256,256]{1,0:T(8,128)S(1)}, f32[256,256]{1,0:T(8,128)S(1)}, u32[]{:S(2)}, u32[]{:S(2)}) %collective-permute-start.41) | collective-permute-done | bytes 262176 | tf_op jit(solution)/shard_map/ppermute | solution.py:418
  271.2 2.9 collective-permute-start.17
  274.1 2.2 collective-permute-done.29.refs_10_
  276.3 2.8 collective-permute-start.19
  279.7 19.3 %collective-permute-done.16.refs_3_ = f32[256,512]{1,0:T(8,128)S(1)} collective-permute-done((f32[256,512]{1,0:T(8,128)}, f32[256,512]{1,0:T(8,128)S(1)}, u32[]{:S(2)}, u32[]{:S(2)}) %collective-permute-start.16) | collective-permute-done | bytes 524320 | tf_op jit(solution)/shard_map/ppermute | solution.py:418
  299.1 2.6 collective-permute-start.31
  301.7 19.6 %collective-permute-done.18.refs_5_ = f32[256,512]{1,0:T(8,128)S(1)} collective-permute-done((f32[256,512]{1,0:T(8,128)}, f32[256,512]{1,0:T(8,128)S(1)}, u32[]{:S(2)}, u32[]{:S(2)}) %collective-permute-start.18) | collective-permute-done | bytes 524320 | tf_op jit(solution)/shard_map/ppermute | solution.py:418
  321.3 2.4 collective-permute-start.33
  323.7 31.7 %collective-permute-done.20.refs_7_ = f32[256,512]{1,0:T(8,128)S(1)} collective-permute-done((f32[256,512]{1,0:T(8,128)}, f32[256,512]{1,0:T(8,128)S(1)}, u32[]{:S(2)}, u32[]{:S(2)}) %collective-permute-start.20) | collective-permute-done | bytes 524320 | tf_op jit(solution)/shard_map/ppermute | solution.py:418
  356.2 15.1 %inverse_x.2 = (f32[1,512,4096]{2,1,0:T(8,128)}, f32[1,512,4096]{2,1,0:T(8,128)}, f32[2,32,512]{2,1,0:T(8,128)}, f32[8,4096]{1,0:T(8,128)}, f32[8,4096]{1,0:T(8,128)}) custom-call(s32[1]{0:T(128)} %bitcast.me_ref, s32[2]{0:T(128)} %offsets_ref.3, f32[256,512]{1,0:T(8,128)} %get-tuple-element.109.refs_0_, f32[256,512]{1,0:T(8,128)} %copy-done.18, ...), custom_call_target="tpu_custom_call" | custom-call | flops 20700000256 | bytes 8388608 | tf_op jit(solution)/shard_map/inverse_x/pallas_call | solution.py:572
  372.0 1.5 collective-permute-start.42
  373.5 4.3 %collective-permute-done.34.refs_15_ = f32[256,256]{1,0:T(8,128)} collective-permute-done((f32[256,256]{1,0:T(8,128)S(1)}, f32[256,256]{1,0:T(8,128)}, u32[]{:S(2)}, u32[]{:S(2)}) %collective-permute-start.34) | collective-permute-done | bytes 262176 | tf_op jit(solution)/shard_map/ppermute | solution.py:418
  378.5 15.6 %inverse_x.3 = (f32[1,512,4096]{2,1,0:T(8,128)}, f32[1,512,4096]{2,1,0:T(8,128)}, f32[2,48,512]{2,1,0:T(8,128)}, f32[8,4096]{1,0:T(8,128)}, f32[8,4096]{1,0:T(8,128)}) custom-call(s32[1]{0:T(128)} %bitcast.me_ref, s32[2]{0:T(128)} %offsets_ref.3, f32[256,512]{1,0:T(8,128)} %get-tuple-element.109.refs_0_, ...), custom_call_target="tpu_custom_call", output_to_operand_aliasing={{0}: (21, {}), {1}: (22, {})} | custom-call | flops 20700000256 | bytes 8388608 | tf_op jit(solution)/shard_map/inverse_x/pallas_call | solution.py:572
  395.2 1.6 collective-permute-start.43
  396.8 1.5 collective-permute-start.44
  398.8 1.4 collective-permute-done.43
  400.2 1.3 collective-permute-done.44
  401.5 2.1 collective-permute-done.45
  (151 shorter events, 9.1 us)
Async XLA Ops:
  7.2 5.8 %collective-permute-start = (f32[512,128]{1,0:T(8,128)}, f32[512,128]{1,0:T(8,128)S(1)}, u32[]{:S(2)}, u32[]{:S(2)}) collective-permute-start(f32[512,128]{1,0:T(8,128)} %get-tuple-element.77), channel_id=1, source_target_pairs={{0,1},{1,0},{2,3},{3,2},{4,5},{5,4},{6,7},{7,6},{8,9},{9,8},{10,11... | collective-permute-start | bytes 786440 | tf_op jit(solution)/shard_map/ppermute | solution.py:418
  7.6 19.9 %collective-permute-start.1 = (f32[512,128]{1,0:T(8,128)}, f32[512,128]{1,0:T(8,128)S(1)}, u32[]{:S(2)}, u32[]{:S(2)}) collective-permute-start(f32[512,128]{1,0:T(8,128)} %get-tuple-element.78), channel_id=1, source_target_pairs={{0,5},{1,4},{2,7},{3,6},{4,1},{5,0},{6,3},{7,2},{8,13},{9,12},{10,... | collective-permute-start | bytes 786440 | tf_op jit(solution)/shard_map/ppermute | solution.py:418
  11.3 17.3 %collective-permute-start.2 = (f32[512,128]{1,0:T(8,128)}, f32[512,128]{1,0:T(8,128)S(1)}, u32[]{:S(2)}, u32[]{:S(2)}) collective-permute-start(f32[512,128]{1,0:T(8,128)} %get-tuple-element.79), channel_id=1, source_target_pairs={{0,2},{1,3},{2,0},{3,1},{4,6},{5,7},{6,4},{7,5},{8,10},{9,11},{10,... | collective-permute-start | bytes 786440 | tf_op jit(solution)/shard_map/ppermute | solution.py:418
  12.9 18.4 %collective-permute-start.3 = (f32[512,128]{1,0:T(8,128)}, f32[512,128]{1,0:T(8,128)S(1)}, u32[]{:S(2)}, u32[]{:S(2)}) collective-permute-start(f32[512,128]{1,0:T(8,128)} %get-tuple-element.80), channel_id=1, source_target_pairs={{0,6},{1,7},{2,4},{3,5},{4,2},{5,3},{6,0},{7,1},{8,14},{9,15},{10,... | collective-permute-start | bytes 786440 | tf_op jit(solution)/shard_map/ppermute | solution.py:418
  12.9 23.6 %collective-permute-start.4 = (f32[512,128]{1,0:T(8,128)}, f32[512,128]{1,0:T(8,128)S(1)}, u32[]{:S(2)}, u32[]{:S(2)}) collective-permute-start(f32[512,128]{1,0:T(8,128)} %get-tuple-element.81), channel_id=1, source_target_pairs={{0,3},{1,2},{2,1},{3,0},{4,7},{5,6},{6,5},{7,4},{8,11},{9,10},{10,... | collective-permute-start | bytes 786440 | tf_op jit(solution)/shard_map/ppermute | solution.py:418
  12.9 28.7 %collective-permute-start.5 = (f32[512,128]{1,0:T(8,128)}, f32[512,128]{1,0:T(8,128)S(1)}, u32[]{:S(2)}, u32[]{:S(2)}) collective-permute-start(f32[512,128]{1,0:T(8,128)} %get-tuple-element.82), channel_id=1, source_target_pairs={{0,7},{1,6},{2,5},{3,4},{4,3},{5,2},{6,1},{7,0},{8,15},{9,14},{10,... | collective-permute-start | bytes 786440 | tf_op jit(solution)/shard_map/ppermute | solution.py:418
  27.6 64.2 %collective-permute-start.21 = (f32[256,384]{1,0:T(8,128)}, f32[256,384]{1,0:T(8,128)S(1)}, u32[]{:S(2)}, u32[]{:S(2)}) collective-permute-start(f32[256,384]{1,0:T(8,128)} %get-tuple-element.118), channel_id=1, source_target_pairs={{0,1},{1,0},{2,3},{3,2},{4,5},{5,4},{6,7},{7,6},{8,9},{9,8},{10,11... | collective-permute-start | bytes 1179656 | tf_op jit(solution)/shard_map/ppermute | solution.py:418
  28.6 66.1 %collective-permute-start.22 = (f32[256,384]{1,0:T(8,128)}, f32[256,384]{1,0:T(8,128)S(1)}, u32[]{:S(2)}, u32[]{:S(2)}) collective-permute-start(f32[256,384]{1,0:T(8,128)} %get-tuple-element.119), channel_id=1, source_target_pairs={{0,5},{1,4},{2,7},{3,6},{4,1},{5,0},{6,3},{7,2},{8,13},{9,12},{10,... | collective-permute-start | bytes 1179656 | tf_op jit(solution)/shard_map/ppermute | solution.py:418
  31.3 63.9 %collective-permute-start.23 = (f32[256,384]{1,0:T(8,128)}, f32[256,384]{1,0:T(8,128)S(1)}, u32[]{:S(2)}, u32[]{:S(2)}) collective-permute-start(f32[256,384]{1,0:T(8,128)} %get-tuple-element.120), channel_id=1, source_target_pairs={{0,2},{1,3},{2,0},{3,1},{4,6},{5,7},{6,4},{7,5},{8,10},{9,11},{10,... | collective-permute-start | bytes 1179656 | tf_op jit(solution)/shard_map/ppermute | solution.py:418
  36.5 61.7 %collective-permute-start.24 = (f32[256,384]{1,0:T(8,128)}, f32[256,384]{1,0:T(8,128)}, u32[]{:S(2)}, u32[]{:S(2)}) collective-permute-start(f32[256,384]{1,0:T(8,128)} %get-tuple-element.121), channel_id=1, source_target_pairs={{0,6},{1,7},{2,4},{3,5},{4,2},{5,3},{6,0},{7,1},{8,14},{9,15},{10,... | collective-permute-start | bytes 1179656 | tf_op jit(solution)/shard_map/ppermute | solution.py:418
  41.6 49.9 %collective-permute-start.6 = (f32[512,128]{1,0:T(8,128)S(1)}, f32[512,128]{1,0:T(8,128)S(1)}, u32[]{:S(2)}, u32[]{:S(2)}) collective-permute-start(f32[512,128]{1,0:T(8,128)S(1)} %copy-done.45), channel_id=1, source_target_pairs={{0,4},{1,5},{2,6},{3,7},{4,0},{5,1},{6,2},{7,3},{8,12},{9,13},{10,... | collective-permute-start | bytes 786440 | tf_op jit(solution)/shard_map/ppermute | solution.py:418
  91.5 39.1 %collective-permute-start.25 = (f32[256,384]{1,0:T(8,128)}, f32[256,384]{1,0:T(8,128)}, u32[]{:S(2)}, u32[]{:S(2)}) collective-permute-start(f32[256,384]{1,0:T(8,128)} %get-tuple-element.122), channel_id=1, source_target_pairs={{0,3},{1,2},{2,1},{3,0},{4,7},{5,6},{6,5},{7,4},{8,11},{9,10},{10,... | collective-permute-start | bytes 1179656 | tf_op jit(solution)/shard_map/ppermute | solution.py:418
  91.7 39.5 %collective-permute-start.26 = (f32[256,384]{1,0:T(8,128)}, f32[256,384]{1,0:T(8,128)}, u32[]{:S(2)}, u32[]{:S(2)}) collective-permute-start(f32[256,384]{1,0:T(8,128)} %get-tuple-element.123), channel_id=1, source_target_pairs={{0,7},{1,6},{2,5},{3,4},{4,3},{5,2},{6,1},{7,0},{8,15},{9,14},{10,... | collective-permute-start | bytes 1179656 | tf_op jit(solution)/shard_map/ppermute | solution.py:418
  94.6 61.3 %collective-permute-start.27 = (f32[256,384]{1,0:T(8,128)}, f32[256,384]{1,0:T(8,128)}, u32[]{:S(2)}, u32[]{:S(2)}) collective-permute-start(f32[256,384]{1,0:T(8,128)} %get-tuple-element.124), channel_id=1, source_target_pairs={{0,4},{1,5},{2,6},{3,7},{4,0},{5,1},{6,2},{7,3},{8,12},{9,13},{10,... | collective-permute-start | bytes 1179656 | tf_op jit(solution)/shard_map/ppermute | solution.py:418
  95.2 60.8 %collective-permute-start.10 = (f32[256,384]{1,0:T(8,128)}, f32[256,384]{1,0:T(8,128)S(1)}, u32[]{:S(2)}, u32[]{:S(2)}) collective-permute-start(f32[256,384]{1,0:T(8,128)} %get-tuple-element.104), channel_id=1, source_target_pairs={{0,6},{1,7},{2,4},{3,5},{4,2},{5,3},{6,0},{7,1},{8,14},{9,15},{10,... | collective-permute-start | bytes 1179656 | tf_op jit(solution)/shard_map/ppermute | solution.py:418
  98.1 66.7 %collective-permute-start.11 = (f32[256,384]{1,0:T(8,128)}, f32[256,384]{1,0:T(8,128)S(1)}, u32[]{:S(2)}, u32[]{:S(2)}) collective-permute-start(f32[256,384]{1,0:T(8,128)} %get-tuple-element.105), channel_id=1, source_target_pairs={{0,3},{1,2},{2,1},{3,0},{4,7},{5,6},{6,5},{7,4},{8,11},{9,10},{10,... | collective-permute-start | bytes 1179656 | tf_op jit(solution)/shard_map/ppermute | solution.py:418
  130.6 50.0 %collective-permute-start.12 = (f32[256,384]{1,0:T(8,128)S(1)}, f32[256,384]{1,0:T(8,128)S(1)}, u32[]{:S(2)}, u32[]{:S(2)}) collective-permute-start(f32[256,384]{1,0:T(8,128)S(1)} %copy-done.29), channel_id=1, source_target_pairs={{0,7},{1,6},{2,5},{3,4},{4,3},{5,2},{6,1},{7,0},{8,15},{9,14},{10,... | collective-permute-start | bytes 1179656 | tf_op jit(solution)/shard_map/ppermute | solution.py:418
  131.3 58.3 %collective-permute-start.13 = (f32[256,384]{1,0:T(8,128)S(1)}, f32[256,384]{1,0:T(8,128)S(1)}, u32[]{:S(2)}, u32[]{:S(2)}) collective-permute-start(f32[256,384]{1,0:T(8,128)S(1)} %copy-done.28), channel_id=1, source_target_pairs={{0,4},{1,5},{2,6},{3,7},{4,0},{5,1},{6,2},{7,3},{8,12},{9,13},{10,... | collective-permute-start | bytes 1179656 | tf_op jit(solution)/shard_map/ppermute | solution.py:418
  156.0 33.6 %collective-permute-start.7 = (f32[256,384]{1,0:T(8,128)S(1)}, f32[256,384]{1,0:T(8,128)S(1)}, u32[]{:S(2)}, u32[]{:S(2)}) collective-permute-start(f32[256,384]{1,0:T(8,128)S(1)} %copy-done.27), channel_id=1, source_target_pairs={{0,1},{1,0},{2,3},{3,2},{4,5},{5,4},{6,7},{7,6},{8,9},{9,8},{10,11... | collective-permute-start | bytes 1179656 | tf_op jit(solution)/shard_map/ppermute | solution.py:418
  156.0 47.3 %collective-permute-start.8 = (f32[256,384]{1,0:T(8,128)S(1)}, f32[256,384]{1,0:T(8,128)S(1)}, u32[]{:S(2)}, u32[]{:S(2)}) collective-permute-start(f32[256,384]{1,0:T(8,128)S(1)} %copy-done.26), channel_id=1, source_target_pairs={{0,5},{1,4},{2,7},{3,6},{4,1},{5,0},{6,3},{7,2},{8,13},{9,12},{10,... | collective-permute-start | bytes 1179656 | tf_op jit(solution)/shard_map/ppermute | solution.py:418
  164.9 40.6 %collective-permute-start.9 = (f32[256,384]{1,0:T(8,128)S(1)}, f32[256,384]{1,0:T(8,128)S(1)}, u32[]{:S(2)}, u32[]{:S(2)}) collective-permute-start(f32[256,384]{1,0:T(8,128)S(1)} %copy-done.25), channel_id=1, source_target_pairs={{0,2},{1,3},{2,0},{3,1},{4,6},{5,7},{6,4},{7,5},{8,10},{9,11},{10,... | collective-permute-start | bytes 1179656 | tf_op jit(solution)/shard_map/ppermute | solution.py:418
  180.6 24.9 %collective-permute-start.35 = (f32[256,256]{1,0:T(8,128)}, f32[256,256]{1,0:T(8,128)S(1)}, u32[]{:S(2)}, u32[]{:S(2)}) collective-permute-start(f32[256,256]{1,0:T(8,128)} %get-tuple-element.134), channel_id=1, source_target_pairs={{0,1},{1,0},{2,3},{3,2},{4,5},{5,4},{6,7},{7,6},{8,9},{9,8},{10,11... | collective-permute-start | bytes 786440 | tf_op jit(solution)/shard_map/ppermute | solution.py:418
  189.6 33.1 %collective-permute-start.36 = (f32[256,256]{1,0:T(8,128)}, f32[256,256]{1,0:T(8,128)S(1)}, u32[]{:S(2)}, u32[]{:S(2)}) collective-permute-start(f32[256,256]{1,0:T(8,128)} %get-tuple-element.135), channel_id=1, source_target_pairs={{0,5},{1,4},{2,7},{3,6},{4,1},{5,0},{6,3},{7,2},{8,13},{9,12},{10,... | collective-permute-start | bytes 786440 | tf_op jit(solution)/shard_map/ppermute | solution.py:418
  189.6 33.5 %collective-permute-start.37 = (f32[256,256]{1,0:T(8,128)}, f32[256,256]{1,0:T(8,128)S(1)}, u32[]{:S(2)}, u32[]{:S(2)}) collective-permute-start(f32[256,256]{1,0:T(8,128)} %get-tuple-element.136), channel_id=1, source_target_pairs={{0,2},{1,3},{2,0},{3,1},{4,6},{5,7},{6,4},{7,5},{8,10},{9,11},{10,... | collective-permute-start | bytes 786440 | tf_op jit(solution)/shard_map/ppermute | solution.py:418
  203.3 21.9 %collective-permute-start.38 = (f32[256,256]{1,0:T(8,128)}, f32[256,256]{1,0:T(8,128)S(1)}, u32[]{:S(2)}, u32[]{:S(2)}) collective-permute-start(f32[256,256]{1,0:T(8,128)} %get-tuple-element.137), channel_id=1, source_target_pairs={{0,6},{1,7},{2,4},{3,5},{4,2},{5,3},{6,0},{7,1},{8,14},{9,15},{10,... | collective-permute-start | bytes 786440 | tf_op jit(solution)/shard_map/ppermute | solution.py:418
  205.5 22.7 %collective-permute-start.39 = (f32[256,256]{1,0:T(8,128)}, f32[256,256]{1,0:T(8,128)S(1)}, u32[]{:S(2)}, u32[]{:S(2)}) collective-permute-start(f32[256,256]{1,0:T(8,128)} %get-tuple-element.138), channel_id=1, source_target_pairs={{0,3},{1,2},{2,1},{3,0},{4,7},{5,6},{6,5},{7,4},{8,11},{9,10},{10,... | collective-permute-start | bytes 786440 | tf_op jit(solution)/shard_map/ppermute | solution.py:418
  205.5 149.8 %copy-start.30 = (f32[256,256]{1,0:T(8,128)S(1)}, f32[256,256]{1,0:T(8,128)}, u32[]{:S(2)}) copy-start(f32[256,256]{1,0:T(8,128)} %get-tuple-element.132) | copy-start | bytes 786436
  205.6 22.7 %collective-permute-start.40 = (f32[256,256]{1,0:T(8,128)}, f32[256,256]{1,0:T(8,128)S(1)}, u32[]{:S(2)}, u32[]{:S(2)}) collective-permute-start(f32[256,256]{1,0:T(8,128)} %get-tuple-element.139), channel_id=1, source_target_pairs={{0,7},{1,6},{2,5},{3,4},{4,3},{5,2},{6,1},{7,0},{8,15},{9,14},{10,... | collective-permute-start | bytes 786440 | tf_op jit(solution)/shard_map/ppermute | solution.py:418
  222.7 132.7 %copy-start.33 = (f32[256,256]{1,0:T(8,128)}, f32[256,256]{1,0:T(8,128)S(1)}, u32[]{:S(2)}) copy-start(f32[256,256]{1,0:T(8,128)S(1)} %collective-permute-done.36.refs_10_) | copy-start | bytes 786436
  222.7 53.6 %collective-permute-start.14 = (f32[256,512]{1,0:T(8,128)}, f32[256,512]{1,0:T(8,128)S(1)}, u32[]{:S(2)}, u32[]{:S(2)}) collective-permute-start(f32[256,512]{1,0:T(8,128)} %get-tuple-element.110), channel_id=1, source_target_pairs={{0,1},{1,0},{2,3},{3,2},{4,5},{5,4},{6,7},{7,6},{8,9},{9,8},{10,11... | collective-permute-start | bytes 1572872 | tf_op jit(solution)/shard_map/ppermute | solution.py:418
  223.1 56.1 %collective-permute-start.15 = (f32[256,512]{1,0:T(8,128)}, f32[256,512]{1,0:T(8,128)S(1)}, u32[]{:S(2)}, u32[]{:S(2)}) collective-permute-start(f32[256,512]{1,0:T(8,128)} %get-tuple-element.111), channel_id=1, source_target_pairs={{0,5},{1,4},{2,7},{3,6},{4,1},{5,0},{6,3},{7,2},{8,13},{9,12},{10,... | collective-permute-start | bytes 1572872 | tf_op jit(solution)/shard_map/ppermute | solution.py:418
  225.2 45.9 %collective-permute-start.41 = (f32[256,256]{1,0:T(8,128)S(1)}, f32[256,256]{1,0:T(8,128)S(1)}, u32[]{:S(2)}, u32[]{:S(2)}) collective-permute-start(f32[256,256]{1,0:T(8,128)S(1)} %copy-done.42), channel_id=1, source_target_pairs={{0,4},{1,5},{2,6},{3,7},{4,0},{5,1},{6,2},{7,3},{8,12},{9,13},{10,... | collective-permute-start | bytes 786440 | tf_op jit(solution)/shard_map/ppermute | solution.py:418
  228.2 43.0 %collective-permute-start.28 = (f32[256,256]{1,0:T(8,128)S(1)}, f32[256,256]{1,0:T(8,128)S(1)}, u32[]{:S(2)}, u32[]{:S(2)}) collective-permute-start(f32[256,256]{1,0:T(8,128)S(1)} %copy-done.41), channel_id=1, source_target_pairs={{0,1},{1,0},{2,3},{3,2},{4,5},{5,4},{6,7},{7,6},{8,9},{9,8},{10,11... | collective-permute-start | bytes 786440 | tf_op jit(solution)/shard_map/ppermute | solution.py:418
  228.3 48.1 %collective-permute-start.29 = (f32[256,256]{1,0:T(8,128)S(1)}, f32[256,256]{1,0:T(8,128)S(1)}, u32[]{:S(2)}, u32[]{:S(2)}) collective-permute-start(f32[256,256]{1,0:T(8,128)S(1)} %copy-done.40), channel_id=1, source_target_pairs={{0,5},{1,4},{2,7},{3,6},{4,1},{5,0},{6,3},{7,2},{8,13},{9,12},{10,... | collective-permute-start | bytes 786440 | tf_op jit(solution)/shard_map/ppermute | solution.py:418
  271.1 28.0 %collective-permute-start.16 = (f32[256,512]{1,0:T(8,128)}, f32[256,512]{1,0:T(8,128)S(1)}, u32[]{:S(2)}, u32[]{:S(2)}) collective-permute-start(f32[256,512]{1,0:T(8,128)} %get-tuple-element.112), channel_id=1, source_target_pairs={{0,2},{1,3},{2,0},{3,1},{4,6},{5,7},{6,4},{7,5},{8,10},{9,11},{10,... | collective-permute-start | bytes 1572872 | tf_op jit(solution)/shard_map/ppermute | solution.py:418
  271.2 27.8 %collective-permute-start.17 = (f32[256,512]{1,0:T(8,128)}, f32[256,512]{1,0:T(8,128)S(1)}, u32[]{:S(2)}, u32[]{:S(2)}) collective-permute-start(f32[256,512]{1,0:T(8,128)} %get-tuple-element.113), channel_id=1, source_target_pairs={{0,6},{1,7},{2,4},{3,5},{4,2},{5,3},{6,0},{7,1},{8,14},{9,15},{10,... | collective-permute-start | bytes 1572872 | tf_op jit(solution)/shard_map/ppermute | solution.py:418
  276.3 45.0 %collective-permute-start.18 = (f32[256,512]{1,0:T(8,128)}, f32[256,512]{1,0:T(8,128)S(1)}, u32[]{:S(2)}, u32[]{:S(2)}) collective-permute-start(f32[256,512]{1,0:T(8,128)} %get-tuple-element.114), channel_id=1, source_target_pairs={{0,3},{1,2},{2,1},{3,0},{4,7},{5,6},{6,5},{7,4},{8,11},{9,10},{10,... | collective-permute-start | bytes 1572872 | tf_op jit(solution)/shard_map/ppermute | solution.py:418
  276.3 45.0 %collective-permute-start.19 = (f32[256,512]{1,0:T(8,128)}, f32[256,512]{1,0:T(8,128)S(1)}, u32[]{:S(2)}, u32[]{:S(2)}) collective-permute-start(f32[256,512]{1,0:T(8,128)} %get-tuple-element.115), channel_id=1, source_target_pairs={{0,7},{1,6},{2,5},{3,4},{4,3},{5,2},{6,1},{7,0},{8,15},{9,14},{10,... | collective-permute-start | bytes 1572872 | tf_op jit(solution)/shard_map/ppermute | solution.py:418
  279.2 76.2 %collective-permute-start.20 = (f32[256,512]{1,0:T(8,128)}, f32[256,512]{1,0:T(8,128)S(1)}, u32[]{:S(2)}, u32[]{:S(2)}) collective-permute-start(f32[256,512]{1,0:T(8,128)} %get-tuple-element.116), channel_id=1, source_target_pairs={{0,4},{1,5},{2,6},{3,7},{4,0},{5,1},{6,2},{7,3},{8,12},{9,13},{10,... | collective-permute-start | bytes 1572872 | tf_op jit(solution)/shard_map/ppermute | solution.py:418
  299.0 72.3 %collective-permute-start.30 = (f32[256,256]{1,0:T(8,128)S(1)}, f32[256,256]{1,0:T(8,128)S(1)}, u32[]{:S(2)}, u32[]{:S(2)}) collective-permute-start(f32[256,256]{1,0:T(8,128)S(1)} %copy-done.31), channel_id=1, source_target_pairs={{0,2},{1,3},{2,0},{3,1},{4,6},{5,7},{6,4},{7,5},{8,10},{9,11},{10,... | collective-permute-start | bytes 786440 | tf_op jit(solution)/shard_map/ppermute | solution.py:418
  299.1 74.5 %collective-permute-start.31 = (f32[256,256]{1,0:T(8,128)}, f32[256,256]{1,0:T(8,128)}, u32[]{:S(2)}, u32[]{:S(2)}) collective-permute-start(f32[256,256]{1,0:T(8,128)} %get-tuple-element.129), channel_id=1, source_target_pairs={{0,6},{1,7},{2,4},{3,5},{4,2},{5,3},{6,0},{7,1},{8,14},{9,15},{10,... | collective-permute-start | bytes 786440 | tf_op jit(solution)/shard_map/ppermute | solution.py:418
  321.3 52.2 %collective-permute-start.32 = (f32[256,256]{1,0:T(8,128)}, f32[256,256]{1,0:T(8,128)}, u32[]{:S(2)}, u32[]{:S(2)}) collective-permute-start(f32[256,256]{1,0:T(8,128)} %get-tuple-element.130), channel_id=1, source_target_pairs={{0,3},{1,2},{2,1},{3,0},{4,7},{5,6},{6,5},{7,4},{8,11},{9,10},{10,... | collective-permute-start | bytes 786440 | tf_op jit(solution)/shard_map/ppermute | solution.py:418
  321.3 52.2 %collective-permute-start.33 = (f32[256,256]{1,0:T(8,128)}, f32[256,256]{1,0:T(8,128)}, u32[]{:S(2)}, u32[]{:S(2)}) collective-permute-start(f32[256,256]{1,0:T(8,128)} %get-tuple-element.131), channel_id=1, source_target_pairs={{0,7},{1,6},{2,5},{3,4},{4,3},{5,2},{6,1},{7,0},{8,15},{9,14},{10,... | collective-permute-start | bytes 786440 | tf_op jit(solution)/shard_map/ppermute | solution.py:418
  355.4 22.5 %collective-permute-start.34 = (f32[256,256]{1,0:T(8,128)S(1)}, f32[256,256]{1,0:T(8,128)}, u32[]{:S(2)}, u32[]{:S(2)}) collective-permute-start(f32[256,256]{1,0:T(8,128)S(1)} %copy-done.30), channel_id=1, source_target_pairs={{0,4},{1,5},{2,6},{3,7},{4,0},{5,1},{6,2},{7,3},{8,12},{9,13},{10,... | collective-permute-start | bytes 786440 | tf_op jit(solution)/shard_map/ppermute | solution.py:418
  372.0 5.8 %collective-permute-start.42 = (f32[8,4096]{1,0:T(8,128)}, f32[8,4096]{1,0:T(8,128)S(1)}, u32[]{:S(2)}, u32[]{:S(2)}) collective-permute-start(f32[8,4096]{1,0:T(8,128)} %get-tuple-element.142), channel_id=1, source_target_pairs={{0,7},{1,0},{2,1},{3,2},{4,3},{5,4},{6,5},{7,6},{8,15},{9,8},{10,9... | collective-permute-start | bytes 393224 | tf_op jit(solution)/shard_map/ppermute | solution.py:676
  395.2 5.0 %collective-permute-start.43 = (f32[2,64,128]{2,1,0:T(8,128)S(1)}, f32[2,64,128]{2,1,0:T(8,128)S(1)}, u32[]{:S(2)}, u32[]{:S(2)}) collective-permute-start(f32[2,64,128]{2,1,0:T(8,128)S(1)} %get-tuple-element.149), channel_id=1, source_target_pairs={{0,8},{8,0},{16,24},{24,16},{1,9},{9,1},{17,25},{25,17},{2,10},{10... | collective-permute-start | bytes 196616 | tf_op jit(solution)/shard_map/ppermute | solution.py:624
  396.8 4.7 %collective-permute-start.44 = (f32[2,64,128]{2,1,0:T(8,128)S(1)}, f32[2,64,128]{2,1,0:T(8,128)S(1)}, u32[]{:S(2)}, u32[]{:S(2)}) collective-permute-start(f32[2,64,128]{2,1,0:T(8,128)S(1)} %get-tuple-element.150), channel_id=1, source_target_pairs={{0,16},{8,24},{16,0},{24,8},{1,17},{9,25},{17,1},{25,9},{2,18},{10... | collective-permute-start | bytes 196616 | tf_op jit(solution)/shard_map/ppermute | solution.py:624
  398.3 5.4 %collective-permute-start.45 = (f32[2,64,128]{2,1,0:T(8,128)S(1)}, f32[2,64,128]{2,1,0:T(8,128)S(1)}, u32[]{:S(2)}, u32[]{:S(2)}) collective-permute-start(f32[2,64,128]{2,1,0:T(8,128)S(1)} %get-tuple-element.151), channel_id=1, source_target_pairs={{0,24},{8,16},{16,8},{24,0},{1,25},{9,17},{17,9},{25,1},{2,26},{10... | collective-permute-start | bytes 196616 | tf_op jit(solution)/shard_map/ppermute | solution.py:624
  (45 other events, 2072.5 us)
